TPU v7x, 256 devices: a whole 4x4x8 slice. The times are simulated.
256 devices in a mesh: section: 32 (over z_hi, y, x), tensor: 8 (over z_lo, core).
Axes of the slice: x: 4, y: 4, z: 8 (z_hi: 2, z_lo: 4; z = z_hi * 4 + z_lo), core: 2. Of those that a mesh axis runs over, the one named last changes fastest.
Arguments:
- x_fwd: bfloat16 [32, 256, 4096], P('section', 'tensor'), may hold values from -6 to 6
- grad_in: bfloat16 [32, 256, 4096], P('section', 'tensor'), may hold values from -6 to 6
- stash: bfloat16 [32, 2, 256, 4096], P('section', None, 'tensor'), may hold values from -6 to 6
- norm_gain: float32 [32, 4096], P('section'), may hold values from 0.25 to 1.75
- w_query: bfloat16 [32, 4096, 4096], P('section', None, 'tensor')
- w_keyval: bfloat16 [32, 2, 4096, 1024], P('section', None, None, 'tensor')
- w_out: bfloat16 [32, 4096, 4096], P('section', 'tensor'), may hold values from -0.09375 to 0.09375
- slot_table: int32 [32, 2], P('section'), may hold values from 0 to 1
Outputs:
- fwd_out: bfloat16 [32, 256, 4096], P('section', 'tensor')
- bwd_out: bfloat16 [32, 256, 4096], P('section', 'tensor')
- stash_out: bfloat16 [32, 2, 256, 4096], P('section', None, 'tensor')
All inputs are finite; a program needn't handle non-finite values.
Results may differ from a plain program's by a relative error of at most 0.02.
The roundings to bfloat16 on the way count: a program that leaves them out, or rounds other values in their place, can miss the bound.
Values may be sent and summed in bfloat16 or wider, within the bound.
No kernel may reach another device: no remote copies, remote signals or barrier semaphores. Data moves between devices by JAX's collectives and lax.ppermute only.
A program may use at most 128 MiB of HBM per device.

v0:
```python
import jax
import jax.numpy as jnp
from jax import lax
from jax.sharding import PartitionSpec as P

HEAD_DIM = 128


EPS = 1e-05
THETA = 500000.0


def from_partner(value, axis, stride):
    mask = 2**stride
    pairs = [(source, source ^ mask) for source in range(lax.axis_size(axis))]
    return lax.ppermute(value, axis, pairs)


def shifted(value, axis, steps):
    count = lax.axis_size(axis)
    leading, last = (max(0, -steps), min(count, count - steps))
    return lax.ppermute(value, axis, [(source, source + steps) for source in range(leading, last)])


def rope_tables(tokens, head_size):
    position = jnp.arange(tokens, dtype=jnp.int32).astype(jnp.float32)
    halfway = head_size // 2
    freq = THETA ** (-2.0 * jnp.arange(halfway, dtype=jnp.float32) / head_size)
    angle = position[:, None] * freq[None, :]
    return (jnp.cos(angle), jnp.sin(angle))


def rotate(values, cosine, sine):
    halfway = values.shape[-1] // 2
    first = values[..., :halfway]
    second = values[..., halfway:]
    cos_rows = cosine[:, None, :]
    sin_rows = sine[:, None, :]
    return jnp.concatenate(
        [first * cos_rows - second * sin_rows, second * cos_rows + first * sin_rows], axis=-1
    )


def normalize(block, gain):
    wide = block.astype(jnp.float32)
    scale = lax.rsqrt(jnp.mean(wide * wide, axis=-1, keepdims=True) + EPS)
    unit = wide * scale
    return ((unit * gain).astype(jnp.bfloat16), unit, scale)


def shape_heads(query, keys, values, cosine, sine):
    tokens = query.shape[0]
    q_heads = query.shape[1] // HEAD_DIM
    k_heads = keys.shape[1] // HEAD_DIM
    query = rotate(query.reshape(tokens, q_heads, HEAD_DIM), cosine, sine).astype(jnp.bfloat16)
    keys = rotate(keys.reshape(tokens, k_heads, HEAD_DIM), cosine, sine).astype(jnp.bfloat16)
    values = values.reshape(tokens, k_heads, HEAD_DIM).astype(jnp.bfloat16)
    return (query.reshape(tokens, k_heads, q_heads // k_heads, HEAD_DIM), keys, values)


def probabilities(query, keys):
    tokens = query.shape[0]
    scores = jnp.einsum(
        "tkgd,ukd->kgtu", query, keys, preferred_element_type=jnp.float32
    ) * HEAD_DIM ** (-0.5)
    causal = jnp.arange(tokens)[:, None] >= jnp.arange(tokens)[None, :]
    scores = jnp.where(causal, scores, -1e30)
    highest = jnp.max(scores, axis=-1, keepdims=True)
    expo = jnp.exp(scores - highest)
    probs = expo / jnp.sum(expo, axis=-1, keepdims=True)
    return (probs, probs.astype(jnp.bfloat16))


def mix_values(rounded, values):
    mixed = jnp.einsum(
        "kgtu,ukd->tkgd", rounded, values, preferred_element_type=jnp.float32
    ).astype(jnp.bfloat16)
    return mixed.reshape(mixed.shape[0], -1)


def attention_back(query, keys, values, probs, rounded, grad_mixed, cosine, sine):
    tokens, k_heads, group, _ = query.shape
    grad_heads = grad_mixed.reshape(tokens, k_heads, group, HEAD_DIM)
    grad_values = jnp.einsum(
        "kgtu,tkgd->ukd", rounded, grad_heads, preferred_element_type=jnp.float32
    )
    grad_probs = jnp.einsum(
        "tkgd,ukd->kgtu", grad_heads, values, preferred_element_type=jnp.float32
    )
    centre = jnp.sum(probs * grad_probs, axis=-1, keepdims=True)
    grad_scores = (probs * (grad_probs - centre) * HEAD_DIM ** (-0.5)).astype(jnp.bfloat16)
    grad_query = jnp.einsum("kgtu,ukd->tkgd", grad_scores, keys, preferred_element_type=jnp.float32)
    grad_keys = jnp.einsum("kgtu,tkgd->ukd", grad_scores, query, preferred_element_type=jnp.float32)
    grad_query = rotate(grad_query.reshape(tokens, k_heads * group, HEAD_DIM), cosine, -sine)
    grad_keys = rotate(grad_keys, cosine, -sine)
    return (
        grad_query.reshape(tokens, -1).astype(jnp.bfloat16),
        grad_keys.reshape(tokens, -1).astype(jnp.bfloat16),
        grad_values.reshape(tokens, -1).astype(jnp.bfloat16),
    )


def norm_back(grad_normed, unit, scale, gain, upstream):
    weighted = grad_normed * gain
    inner = jnp.mean(weighted * unit, axis=-1, keepdims=True)
    return (upstream.astype(jnp.float32) + scale * (weighted - unit * inner)).astype(jnp.bfloat16)


def body(x_fwd, grad_in, stash, norm_gain, w_query, w_keyval, w_out, slot_table):
    section_idx = lax.axis_index("section")
    sections = lax.axis_size("section")
    is_early = section_idx < sections // 2
    rows = x_fwd.shape[1]
    tokens = rows * lax.axis_size("tensor")
    gain = norm_gain[0]
    weight_q = w_query[0]
    weight_k = w_keyval[0, 0]
    weight_v = w_keyval[0, 1]
    weight_o = w_out[0]
    q_width = weight_q.shape[1]
    k_width = weight_k.shape[1]
    held = stash[0]
    returned = lax.dynamic_index_in_dim(held, slot_table[0, 0], 0, keepdims=False)
    payload = jnp.where(is_early, x_fwd[0], returned)
    levels = sections.bit_length() - 1
    bit_list = list(range(levels))
    for bit_now in bit_list:
        payload = from_partner(payload, "section", bit_now)
    own_block = lax.dynamic_index_in_dim(held, slot_table[0, 1], 0, keepdims=False)
    checkpoint = jnp.where(is_early, payload, own_block)
    slot_ids = jnp.arange(held.shape[0], dtype=jnp.int32)
    replace = jnp.logical_and(slot_ids == slot_table[0, 0], jnp.logical_not(is_early))
    stash_out = jnp.where(replace[:, None, None], payload[None], held)[None]
    normed_fwd, _, _ = normalize(x_fwd[0], gain)
    normed_bwd, unit, scale = normalize(checkpoint, gain)
    both_normed = jnp.stack([normed_fwd, normed_bwd])
    piece = lax.all_gather(both_normed, "tensor", axis=1, tiled=True)
    query_part = jnp.einsum("brd,dq->brq", piece, weight_q, preferred_element_type=jnp.float32)
    keys_part = jnp.einsum("brd,dq->brq", piece, weight_k, preferred_element_type=jnp.float32)
    values_part = jnp.einsum("brd,dq->brq", piece, weight_v, preferred_element_type=jnp.float32)
    projected = jnp.concatenate([query_part, keys_part, values_part], axis=2)
    cosine, sine = rope_tables(tokens, HEAD_DIM)
    query, keys, values = shape_heads(
        projected[0, :, :q_width],
        projected[0, :, q_width : q_width + k_width],
        projected[0, :, q_width + k_width :],
        cosine,
        sine,
    )
    query_b, keys_b, values_b = shape_heads(
        projected[1, :, :q_width],
        projected[1, :, q_width : q_width + k_width],
        projected[1, :, q_width + k_width :],
        cosine,
        sine,
    )
    _, rounded = probabilities(query, keys)
    mixed = mix_values(rounded, values)
    tensor_idx = lax.axis_index("tensor")
    total = lax.psum(
        jnp.dot(mixed, weight_o, preferred_element_type=jnp.float32).astype(jnp.bfloat16), "tensor"
    ).astype(jnp.float32)
    attn_part = lax.dynamic_slice_in_dim(total, tensor_idx * rows, rows, 0)
    output = (x_fwd[0].astype(jnp.float32) + attn_part).astype(jnp.bfloat16)
    fwd_out = shifted(output[None], "section", 1)
    grad_mixed = jnp.einsum(
        "rd,qd->rq",
        lax.all_gather(grad_in[0], "tensor", axis=0, tiled=True),
        weight_o,
        preferred_element_type=jnp.float32,
    ).astype(jnp.bfloat16)
    probs_b, rounded_b = probabilities(query_b, keys_b)
    grad_query, grad_keys, grad_values = attention_back(
        query_b, keys_b, values_b, probs_b, rounded_b, grad_mixed, cosine, sine
    )
    summed = jnp.einsum("tq,dq->td", grad_query, weight_q, preferred_element_type=jnp.float32)
    summed = summed + jnp.einsum(
        "tq,dq->td", grad_keys, weight_k, preferred_element_type=jnp.float32
    )
    total_grad = lax.psum(
        (
            summed
            + jnp.einsum("tq,dq->td", grad_values, weight_v, preferred_element_type=jnp.float32)
        ).astype(jnp.bfloat16),
        "tensor",
    ).astype(jnp.float32)
    grad_normed = lax.dynamic_slice_in_dim(total_grad, tensor_idx * rows, rows, 0)
    grad_x = norm_back(grad_normed, unit, scale, gain, grad_in[0])
    bwd_out = shifted(grad_x[None], "section", -1)
    return (fwd_out, bwd_out, stash_out)


def solution(mesh):
    placed = (
        P("section", "tensor", None),
        P("section", "tensor", None),
        P("section", None, "tensor", None),
        P("section", None),
        P("section", None, "tensor"),
        P("section", None, None, "tensor"),
        P("section", "tensor", None),
        P("section", None),
    )
    return jax.shard_map(
        body,
        mesh=mesh,
        in_specs=placed,
        out_specs=(
            P("section", "tensor", None),
            P("section", "tensor", None),
            P("section", None, "tensor", None),
        ),
        check_vma=False,
    )
```

profile of v0, /device:TPU:193, one launch (start us, length us, event | category | flops | bytes accessed | tf_op | source)
XLA Modules:
  0.0 307.4 jit_solution(9620611100714082721)
XLA Ops:
  7.2 1.3 fusion.103
  11.5 1.3 collective-permute-start
  12.9 5.9 %collective-permute-done = bf16[32,4096]{1,0:T(8,128)(2,1)S(1)} collective-permute-done((bf16[32,4096]{1,0:T(8,128)(2,1)S(1)}, bf16[32,4096]{1,0:T(8,128)(2,1)S(1)}, u32[]{:S(2)}, u32[]{:S(2)}) %collective-permute-start) | collective-permute-done | bytes 262176 | tf_op jit(solution)/shard_map/ppermute | solution.py:16
  18.8 2.7 collective-permute-start.1
  21.5 5.0 %collective-permute-done.1 = bf16[32,4096]{1,0:T(8,128)(2,1)S(1)} collective-permute-done((bf16[32,4096]{1,0:T(8,128)(2,1)S(1)}, bf16[32,4096]{1,0:T(8,128)(2,1)S(1)}, u32[]{:S(2)}, u32[]{:S(2)}) %collective-permute-start.1) | collective-permute-done | bytes 262176 | tf_op jit(solution)/shard_map/ppermute | solution.py:16
  27.8 4.3 %collective-permute-done.2 = bf16[32,4096]{1,0:T(8,128)(2,1)S(1)} collective-permute-done((bf16[32,4096]{1,0:T(8,128)(2,1)S(1)}, bf16[32,4096]{1,0:T(8,128)(2,1)S(1)}, u32[]{:S(2)}, u32[]{:S(2)}) %collective-permute-start.2) | collective-permute-done | bytes 262176 | tf_op jit(solution)/shard_map/ppermute | solution.py:16
  32.1 2.9 collective-permute-start.3
  36.2 4.2 %collective-permute-done.3 = bf16[32,4096]{1,0:T(8,128)(2,1)S(1)} collective-permute-done((bf16[32,4096]{1,0:T(8,128)(2,1)S(1)}, bf16[32,4096]{1,0:T(8,128)(2,1)S(1)}, u32[]{:S(2)}, u32[]{:S(2)}) %collective-permute-start.3) | collective-permute-done | bytes 262176 | tf_op jit(solution)/shard_map/ppermute | solution.py:16
  43.6 14.9 %collective-permute-done.4 = bf16[32,4096]{1,0:T(8,128)(2,1)S(1)} collective-permute-done((bf16[32,4096]{1,0:T(8,128)(2,1)S(1)}, bf16[32,4096]{1,0:T(8,128)(2,1)S(1)}, u32[]{:S(2)}, u32[]{:S(2)}) %collective-permute-start.4) | collective-permute-done | bytes 262176 | tf_op jit(solution)/shard_map/ppermute | solution.py:16
  63.7 4.1 %fusion.12 = bf16[256,512]{1,0:T(8,128)(2,1)S(1)} fusion(bf16[1,512,4096]{2,1,0:T(8,128)(2,1)} %param.14, bf16[1,256,4096]{2,1,0:T(8,128)(2,1)} %all-gather.6.cloned.1.call-done), kind=kOutput, calls=%fused_computation.19 | convolution fusion | flops 1073872896 | bytes 6553600 | tf_op jit(solution)/shard_map/rd,qd->rq/dot_general | solution.py:166
  68.7 48.2 %all-gather.4.cloned.1.call-done = bf16[2,256,4096]{2,1,0:T(8,128)(2,1)} async-done(((bf16[2,32,4096]{2,1,0:T(8,128)(2,1)}), bf16[2,256,4096]{2,1,0:T(8,128)(2,1)}) %all-gather.4.cloned.1.call-update) | async-done | bytes 4194320 | tf_op jit(solution)/shard_map/all_gather | solution.py:137
  116.9 5.8 %fusion.4 = f32[2,256,512]{2,1,0:T(8,128)S(1)} fusion(bf16[2,256,4096]{2,1,0:T(8,128)(2,1)} %all-gather.4.cloned.1.call-done, bf16[1,4096,512]{2,1,0:T(8,128)(2,1)} %param.12), kind=kOutput, calls=%fused_computation.7 | convolution fusion | flops 2147483648 | bytes 9437184 | tf_op jit(solution)/shard_map/brd,dq->brq/dot_general | solution.py:138
  125.0 3.7 %fusion.21 = f32[2,256,128]{1,2,0:T(8,128)S(1)} fusion(bf16[2,256,4096]{2,1,0:T(8,128)(2,1)} %all-gather.4.cloned.1.call-done, bf16[1,2,4096,128]{3,2,1,0:T(8,128)(2,1)S(1)} %copy-done), kind=kOutput, calls=%fused_computation.28 | convolution fusion | flops 536870912 | bytes 5505024 | tf_op jit(solution)/shard_map/brd,dq->brq/dot_general | solution.py:139
  136.9 1.8 copy.39
  138.7 1.4 fusion.92
  141.0 3.3 %convolution_add_fusion = f32[256,4096]{1,0:T(8,128)} fusion(f32[256,4096]{1,0:T(8,128)S(1)} %fusion.19, bf16[256,512]{0,1:T(8,128)(2,1)S(1)} %bitcast.164, bf16[1,4096,512]{2,1,0:T(8,128)(2,1)S(1)} %copy-done.1), kind=kOutput, calls=%fused_computation | convolution fusion | flops 1074790400 | bytes 12845056 | tf_op jit(solution)/shard_map/tq,dq->td/dot_general | solution.py:176
  144.3 5.2 %fusion = bf16[256,4096]{1,0:T(8,128)(2,1)} fusion(f32[256,4096]{1,0:T(8,128)} %convolution_add_fusion, bf16[256,4,128]{0,2,1:T(8,128)(2,1)} %bitcast.162, bf16[1,2,4096,128]{3,2,1,0:T(8,128)(2,1)S(1)} %copy-done, f32[1,4,256,256]{2,3,1,0:T(8,128)S(1)} %get-tuple-element.37, f32[4,256]{1,0:T(4,128)S(1)} %fusion.27, f32[4,256]{1,0:T(4,128)S(1)} %get-tuple-element.36), kind=kOutput, calls=%fused_computation.2 | convolution fusion | flops 338460672 | bytes 8658944 | tf_op jit(solution)/shard_map/tq,dq->td/dot_general | solution.py:183
  149.4 1.6 fusion.105
  152.4 2.7 convolution_convert_fusion
  155.9 108.3 %all-reduce.3.cloned.1.call-done = (bf16[256,4096]{1,0:T(8,128)(2,1)}, bf16[256,4096]{1,0:T(8,128)(2,1)}) async-done(((bf16[256,4096]{1,0:T(8,128)(2,1)}, bf16[256,4096]{1,0:T(8,128)(2,1)}), (bf16[256,4096]{1,0:T(8,128)(2,1)}, bf16[256,4096]{1,0:T(8,128)(2,1)})) %all-reduce.3.cloned.1.call-update) | async-done | bytes 4194320 | tf_op jit(solution)/shard_map/psum | solution.py:160
  266.5 8.6 %collective-permute-start.6 = (bf16[1,32,4096]{2,1,0:T(8,128)(2,1)S(1)}, bf16[1,32,4096]{2,1,0:T(8,128)(2,1)S(1)}, u32[]{:S(2)}, u32[]{:S(2)}) collective-permute-start(bf16[1,32,4096]{2,1,0:T(8,128)(2,1)S(1)} %fusion.50), channel_id=1, source_target_pairs={{8,0},{16,8},{24,16},{32,24},{40,32},{48,40},{56,48},{64,56},{72,6... | collective-permute-start | bytes 786440 | tf_op jit(solution)/shard_map/ppermute | solution.py:22
  276.2 1.9 collective-permute-start.5
  279.0 7.1 %collective-permute-done.6 = bf16[1,32,4096]{2,1,0:T(8,128)(2,1)S(1)} collective-permute-done((bf16[1,32,4096]{2,1,0:T(8,128)(2,1)S(1)}, bf16[1,32,4096]{2,1,0:T(8,128)(2,1)S(1)}, u32[]{:S(2)}, u32[]{:S(2)}) %collective-permute-start.6) | collective-permute-done | bytes 262176 | tf_op jit(solution)/shard_map/ppermute | solution.py:22
  286.2 13.3 %collective-permute-done.5 = bf16[1,32,4096]{2,1,0:T(8,128)(2,1)S(1)} collective-permute-done((bf16[1,32,4096]{2,1,0:T(8,128)(2,1)S(1)}, bf16[1,32,4096]{2,1,0:T(8,128)(2,1)S(1)}, u32[]{:S(2)}, u32[]{:S(2)}) %collective-permute-start.5) | collective-permute-done | bytes 262176 | tf_op jit(solution)/shard_map/ppermute | solution.py:22
  (85 shorter events, 29.9 us)
Async XLA Ops:
  7.2 56.6 %all-gather.6.cloned.1.call-start = ((), (), s32[]{:S(2)}) async-start(), calls=%async_computation.1 | async-start | bytes 2359296 | tf_op jit(solution)/shard_map/all_gather | solution.py:168
  11.5 7.3 %collective-permute-start = (bf16[32,4096]{1,0:T(8,128)(2,1)S(1)}, bf16[32,4096]{1,0:T(8,128)(2,1)S(1)}, u32[]{:S(2)}, u32[]{:S(2)}) collective-permute-start(bf16[32,4096]{1,0:T(8,128)(2,1)S(1)} %bitcast_select_fusion.1), channel_id=1, source_target_pairs={{0,8},{8,0},{16,24},{24,16},{32,40},{40,32},{48,56},{56,48},{64,72... | collective-permute-start | bytes 786440 | tf_op jit(solution)/shard_map/ppermute | solution.py:16
  12.8 104.1 %all-gather.4.cloned.1.call-start = ((), (), s32[]{:S(2)}) async-start(), calls=%async_computation | async-start | bytes 4718592 | tf_op jit(solution)/shard_map/all_gather | solution.py:137
  18.8 7.8 %collective-permute-start.1 = (bf16[32,4096]{1,0:T(8,128)(2,1)S(1)}, bf16[32,4096]{1,0:T(8,128)(2,1)S(1)}, u32[]{:S(2)}, u32[]{:S(2)}) collective-permute-start(bf16[32,4096]{1,0:T(8,128)(2,1)S(1)} %collective-permute-done), channel_id=1, source_target_pairs={{0,16},{8,24},{16,0},{24,8},{32,48},{40,56},{48,32},{56,40},{64,80... | collective-permute-start | bytes 786440 | tf_op jit(solution)/shard_map/ppermute | solution.py:16
  26.5 5.6 %collective-permute-start.2 = (bf16[32,4096]{1,0:T(8,128)(2,1)S(1)}, bf16[32,4096]{1,0:T(8,128)(2,1)S(1)}, u32[]{:S(2)}, u32[]{:S(2)}) collective-permute-start(bf16[32,4096]{1,0:T(8,128)(2,1)S(1)} %collective-permute-done.1), channel_id=1, source_target_pairs={{0,32},{8,40},{16,48},{24,56},{32,0},{40,8},{48,16},{56,24},{64,96... | collective-permute-start | bytes 786440 | tf_op jit(solution)/shard_map/ppermute | solution.py:16
  32.1 8.2 %collective-permute-start.3 = (bf16[32,4096]{1,0:T(8,128)(2,1)S(1)}, bf16[32,4096]{1,0:T(8,128)(2,1)S(1)}, u32[]{:S(2)}, u32[]{:S(2)}) collective-permute-start(bf16[32,4096]{1,0:T(8,128)(2,1)S(1)} %collective-permute-done.2), channel_id=1, source_target_pairs={{0,64},{8,72},{16,80},{24,88},{32,96},{40,104},{48,112},{56,120},{... | collective-permute-start | bytes 786440 | tf_op jit(solution)/shard_map/ppermute | solution.py:16
  40.3 18.2 %collective-permute-start.4 = (bf16[32,4096]{1,0:T(8,128)(2,1)S(1)}, bf16[32,4096]{1,0:T(8,128)(2,1)S(1)}, u32[]{:S(2)}, u32[]{:S(2)}) collective-permute-start(bf16[32,4096]{1,0:T(8,128)(2,1)S(1)} %collective-permute-done.3), channel_id=1, source_target_pairs={{0,128},{8,136},{16,144},{24,152},{32,160},{40,168},{48,176},{56,1... | collective-permute-start | bytes 786440 | tf_op jit(solution)/shard_map/ppermute | solution.py:16
  58.6 9.3 %copy-start.7 = (bf16[32,4096]{1,0:T(8,128)(2,1)}, bf16[32,4096]{1,0:T(8,128)(2,1)S(1)}, u32[]{:S(2)}) copy-start(bf16[32,4096]{1,0:T(8,128)(2,1)S(1)} %collective-permute-done.4) | copy-start | bytes 786436
  61.6 202.6 %all-reduce.3.cloned.1.call-start = ((), (), s32[]{:S(2)}) async-start(), calls=%async_computation.2 | async-start | bytes 8388608 | tf_op jit(solution)/shard_map/psum | solution.py:160
  61.8 67.6 %copy-start.16 = (f32[64]{0:T(128)}, f32[64]{0:T(128)S(1)}, u32[]{:S(2)}) copy-start(f32[64]{0:T(128)S(1)} %multiply_power_fusion) | copy-start | bytes 772
  125.0 5.4 %copy-start.14 = (f32[256,64]{1,0:T(8,128)S(1)}, f32[256,64]{1,0:T(8,128)}, u32[]{:S(2)}) copy-start(f32[256,64]{1,0:T(8,128)} %get-tuple-element.30) | copy-start | bytes 196612
  128.7 2.7 copy-start.11
  129.7 2.4 copy-start.3
  133.4 2.4 copy-start.13
  138.7 2.3 copy-start.10
  144.3 5.2 %copy-start.12 = (pred[256,256]{0,1:T(8,128)(4,1)S(1)}, pred[256,256]{0,1:T(8,128)(4,1)}, u32[]{:S(2)}) copy-start(pred[256,256]{0,1:T(8,128)(4,1)} %iota_compare_fusion) | copy-start | bytes 196612
  149.4 3.0 copy-start.2
  152.4 111.8 %copy-start.15 = (f32[1,4096]{1,0:T(1,128)S(1)}, f32[1,4096]{1,0:T(1,128)}, u32[]{:S(2)}) copy-start(f32[1,4096]{1,0:T(1,128)} %param.11) | copy-start | bytes 49156
  152.4 112.9 %copy-start.6 = (bf16[1,32,4096]{2,1,0:T(8,128)(2,1)S(1)}, bf16[1,32,4096]{2,1,0:T(8,128)(2,1)}, u32[]{:S(2)}) copy-start(bf16[1,32,4096]{2,1,0:T(8,128)(2,1)} %param.9) | copy-start | bytes 786436
  155.1 120.0 %copy-start.4 = (bf16[1,32,4096]{2,1,0:T(8,128)(2,1)S(1)}, bf16[1,32,4096]{2,1,0:T(8,128)(2,1)}, u32[]{:S(2)}) copy-start(bf16[1,32,4096]{2,1,0:T(8,128)(2,1)} %param.8) | copy-start | bytes 786436
  155.1 123.0 %copy-start.5 = (bf16[1,2,32,4096]{3,2,1,0:T(8,128)(2,1)S(1)}, bf16[1,2,32,4096]{3,2,1,0:T(8,128)(2,1)}, u32[]{:S(2)}) copy-start(bf16[1,2,32,4096]{3,2,1,0:T(8,128)(2,1)} %param.10) | copy-start | bytes 1572868
  155.1 123.0 %copy-start.8 = (bf16[32,4096]{1,0:T(8,128)(2,1)S(1)}, bf16[32,4096]{1,0:T(8,128)(2,1)}, u32[]{:S(2)}) copy-start(bf16[32,4096]{1,0:T(8,128)(2,1)} %copy-done.7) | copy-start | bytes 786436
  266.5 19.6 %collective-permute-start.6 = (bf16[1,32,4096]{2,1,0:T(8,128)(2,1)S(1)}, bf16[1,32,4096]{2,1,0:T(8,128)(2,1)S(1)}, u32[]{:S(2)}, u32[]{:S(2)}) collective-permute-start(bf16[1,32,4096]{2,1,0:T(8,128)(2,1)S(1)} %fusion.50), channel_id=1, source_target_pairs={{8,0},{16,8},{24,16},{32,24},{40,32},{48,40},{56,48},{64,56},{72,6... | collective-permute-start | bytes 786440 | tf_op jit(solution)/shard_map/ppermute | solution.py:22
  276.2 23.3 %collective-permute-start.5 = (bf16[1,32,4096]{2,1,0:T(8,128)(2,1)S(1)}, bf16[1,32,4096]{2,1,0:T(8,128)(2,1)S(1)}, u32[]{:S(2)}, u32[]{:S(2)}) collective-permute-start(bf16[1,32,4096]{2,1,0:T(8,128)(2,1)S(1)} %fusion.52), channel_id=1, source_target_pairs={{0,8},{8,16},{16,24},{24,32},{32,40},{40,48},{48,56},{56,64},{64,7... | collective-permute-start | bytes 786440 | tf_op jit(solution)/shard_map/ppermute | solution.py:22
  (4 other events, 7.2 us)
Sparse Core Ops, SparseCore 0:
  12.9 44.3 all-gather.5
  61.7 55.1 all-gather.3
  155.3 108.8 all-reduce.2
where the time goes:
time: 308 us; the launch traced here: 307 us
  waiting for transfers between devices  211 us (69%)
  matrix products  31.7 us (10%)
  starting transfers between devices  19.4 us (6%)
  between operations  17.9 us (6%)
  other arithmetic  17.7 us (6%)
  local copies, waits for them, and re-layouts  9.53 us (3%)
    psum x1, waiting for transfers between devices, body(): lax.psum(jnp.dot(mixed, weight_o, preferred_element_type=jnp.float32).ast...  108 us
    all_gather x1, waiting for transfers between devices, body(): piece = lax.all_gather(both_normed, 'tensor', axis=1, tiled=True)  48.2 us
    ppermute x5, waiting for transfers between devices, from_partner(): return lax.ppermute(value, axis, pairs)  34.3 us
    ppermute x2, waiting for transfers between devices, shifted(): lax.ppermute(value, axis, [(source, source + steps) for source in range(l...  20.5 us
    ppermute x2, starting transfers between devices, shifted(): lax.ppermute(value, axis, [(source, source + steps) for source in range(l...  10.5 us
    ppermute x5, starting transfers between devices, from_partner(): return lax.ppermute(value, axis, pairs)  8.54 us
  transfers between devices with their start and end apart: 10, of which 9 were waited for; matrix products, arithmetic and copies ran while one was open for 5% of the time, Pallas kernels for 0%

commit v1 on v0

v1 whole, which is shorter than its diff:
```python
import jax
import jax.numpy as jnp
from jax import lax
from jax.experimental import pallas as pl
from jax.experimental.pallas import tpu as pltpu
from jax.sharding import PartitionSpec as P

HEAD_DIM = 128
EPS = 1e-05
THETA = 500000.0
CHUNKS = 4
F32 = jnp.float32
BF16 = jnp.bfloat16


def core_swap(value):
    size = lax.axis_size("tensor")
    return lax.ppermute(value, "tensor", [(i, i ^ 1) for i in range(size)])


def chip_swap(value, mask):
    size = lax.axis_size("tensor")
    return lax.ppermute(value, "tensor", [(i, i ^ (2 * mask)) for i in range(size)])


def shifted(value, steps):
    count = lax.axis_size("section")
    return lax.ppermute(
        value, "section", [(i, i + steps) for i in range(count) if 0 <= i + steps < count]
    )


def after(value, *earlier):
    return lax.optimization_barrier((value, *earlier))[0]


def scatter_parts(own, swapped):
    rows = own.shape[0] // 4
    spans = [slice(j * rows, (j + 1) * rows) for j in range(4)]
    return [own[span] + swapped[span].astype(F32) for span in spans]


def local_positions(rows):
    index = lax.axis_index("tensor")
    blocks = [index ^ (2 * j + k) for k in range(2) for j in range(4)]
    start = jnp.stack(blocks) * rows
    return (start[:, None] + jnp.arange(rows, dtype=jnp.int32)[None, :]).reshape(-1)


def rope_tables(position, head_size):
    halfway = head_size // 2
    freq = THETA ** (-2.0 * jnp.arange(halfway, dtype=F32) / head_size)
    angle = position.astype(F32)[:, None] * freq[None, :]
    return (jnp.cos(angle), jnp.sin(angle))


def normalize(block, gain):
    wide = block.astype(F32)
    scale = lax.rsqrt(jnp.mean(wide * wide, axis=-1, keepdims=True) + EPS)
    unit = wide * scale
    return ((unit * gain).astype(BF16), unit, scale)


def swing(values, cosine, sine):
    return values * cosine + pltpu.roll(values, HEAD_DIM // 2, 1) * sine


def dot(left, right, left_dim=1, right_dim=0):
    return lax.dot_general(left, right, (((left_dim,), (right_dim,)), ((), ())), preferred_element_type=F32)


def copy_pieces(pieces, tokens, sems):
    rows = tokens.shape[0] // len(pieces)
    copies = [
        pltpu.make_async_copy(piece, tokens.at[pl.ds(i * rows, rows)], sems.at[i]) for i, piece in enumerate(pieces)
    ]
    for copy in copies:
        copy.start()
    return copies


def qkv_kernel(*refs):
    pieces = refs[:8]
    wq, wkv, cosine, sine, q_out, k_out, v_out, tokens, weights, acc, sems, wsems = refs[8:]
    depth = wq.shape[1] // CHUNKS
    width = wq.shape[2]
    copies = copy_pieces(pieces, tokens, sems)
    loads = []
    for c in range(CHUNKS):
        span = pl.ds(c * depth, depth)
        loads.append(
            [
                pltpu.make_async_copy(wq.at[0, span], weights.at[span, pl.ds(0, width)], wsems.at[c, 0]),
                pltpu.make_async_copy(wkv.at[0, 0, span], weights.at[span, pl.ds(width, HEAD_DIM)], wsems.at[c, 1]),
                pltpu.make_async_copy(
                    wkv.at[0, 1, span], weights.at[span, pl.ds(width + HEAD_DIM, HEAD_DIM)], wsems.at[c, 2]
                ),
            ]
        )
        for load in loads[-1]:
            load.start()
    for copy in copies:
        copy.wait()
    for c in range(CHUNKS):
        for load in loads[c]:
            load.wait()
        part = dot(tokens[:, c * depth : (c + 1) * depth], weights[c * depth : (c + 1) * depth, :])
        if c == 0:
            acc[...] = part
        else:
            acc[...] += part
    cos = cosine[...]
    sin = sine[...]
    for h in range(width // HEAD_DIM):
        cols = slice(h * HEAD_DIM, (h + 1) * HEAD_DIM)
        q_out[:, cols] = swing(acc[:, cols], cos, sin).astype(BF16)
    k_out[...] = swing(acc[:, width : width + HEAD_DIM], cos, sin).astype(BF16)
    v_out[...] = acc[:, width + HEAD_DIM :].astype(BF16)


def head_probs(query, keys, mask):
    scores = dot(query, keys, 1, 1) * HEAD_DIM ** (-0.5)
    scores = jnp.where(mask > 0.0, scores, -1e30)
    expo = jnp.exp(scores - jnp.max(scores, axis=-1, keepdims=True))
    return expo / jnp.sum(expo, axis=-1, keepdims=True)


def attn_fwd_kernel(q, k, v, mask, wo, own_out, other_out, weights, mixed, sems):
    heads = q.shape[1] // HEAD_DIM
    loads = []
    for h in range(heads):
        span = pl.ds(h * HEAD_DIM, HEAD_DIM)
        loads.append(pltpu.make_async_copy(wo.at[0, span], weights.at[span], sems.at[h]))
        loads[-1].start()
    for h in range(heads):
        cols = slice(h * HEAD_DIM, (h + 1) * HEAD_DIM)
        probs = head_probs(q[:, cols], k[...], mask[...])
        mixed[:, cols] = dot(probs.astype(BF16), v[...]).astype(BF16)
    for load in loads:
        load.wait()
    half = q.shape[0] // 2
    step = weights.shape[1] // CHUNKS
    for c in range(CHUNKS):
        cols = slice(c * step, (c + 1) * step)
        part = dot(mixed[...], weights[:, cols])
        own_out[:, cols] = part[:half]
        other_out[:, cols] = part[half:].astype(BF16)


def grad_mixed_kernel(*refs):
    pieces = refs[:8]
    wo, out, tokens, weights, sems, wsems = refs[8:]
    heads = out.shape[1] // HEAD_DIM
    copies = copy_pieces(pieces, tokens, sems)
    loads = []
    for h in range(heads):
        span = pl.ds(h * HEAD_DIM, HEAD_DIM)
        loads.append(pltpu.make_async_copy(wo.at[0, span], weights.at[span], wsems.at[h]))
        loads[-1].start()
    for copy in copies:
        copy.wait()
    for h in range(0, heads, 2):
        loads[h].wait()
        loads[h + 1].wait()
        cols = slice(h * HEAD_DIM, (h + 2) * HEAD_DIM)
        out[:, cols] = dot(tokens[...], weights[cols, :], 1, 1).astype(BF16)


def attn_bwd_kernel(q, k, v, gm, mask, cosine, sine, gq_out, gk_out, gv_out):
    heads = q.shape[1] // HEAD_DIM
    cos = cosine[...]
    sin = -sine[...]
    keys = k[...]
    values = v[...]
    grad_keys = None
    for h in range(heads):
        cols = slice(h * HEAD_DIM, (h + 1) * HEAD_DIM)
        query = q[:, cols]
        grad = gm[:, cols]
        probs = head_probs(query, keys, mask[...])
        grad_probs = dot(grad, values, 1, 1)
        centre = jnp.sum(probs * grad_probs, axis=-1, keepdims=True)
        grad_scores = (probs * (grad_probs - centre) * HEAD_DIM ** (-0.5)).astype(BF16)
        gq_out[:, cols] = swing(dot(grad_scores, keys), cos, sin).astype(BF16)
        more_keys = dot(grad_scores, query, 0, 0)
        more_values = dot(probs.astype(BF16), grad, 0, 0)
        grad_keys = more_keys if grad_keys is None else grad_keys + more_keys
        grad_values = more_values if h == 0 else grad_values + more_values
    gk_out[...] = swing(grad_keys, cos, sin).astype(BF16)
    gv_out[...] = grad_values.astype(BF16)


def call(kernel, outs, moved, hbm, vmem, scratch, flops):
    return pl.pallas_call(
        kernel,
        out_shape=[jax.ShapeDtypeStruct(shape, dtype) for shape, dtype in outs],
        in_specs=[pl.BlockSpec(memory_space=pl.ANY)] * len(moved) + [pl.BlockSpec(memory_space=pltpu.HBM)] * len(hbm) + [pl.BlockSpec(memory_space=pltpu.VMEM)] * len(vmem),
        out_specs=[pl.BlockSpec(memory_space=pltpu.VMEM)] * len(outs),
        scratch_shapes=scratch,
        compiler_params=pltpu.CompilerParams(vmem_limit_bytes=40 * 1024 * 1024),
        cost_estimate=pl.CostEstimate(flops=flops // 64, bytes_accessed=65536, transcendentals=0),
    )(*moved, *hbm, *vmem)


def qkv(pieces, w_query, w_keyval, cosine, sine):
    tokens = 8 * pieces[0].shape[0]
    depth, width = w_query.shape[1:]
    full = width + 2 * HEAD_DIM
    return call(
        qkv_kernel,
        [((tokens, width), BF16), ((tokens, HEAD_DIM), BF16), ((tokens, HEAD_DIM), BF16)],
        pieces,
        [w_query, w_keyval],
        [cosine, sine],
        [
            pltpu.VMEM((tokens, depth), BF16),
            pltpu.VMEM((depth, full), BF16),
            pltpu.VMEM((tokens, full), F32),
            pltpu.SemaphoreType.DMA((8,)),
            pltpu.SemaphoreType.DMA((CHUNKS, 3)),
        ],
        2 * tokens * depth * full,
    )


def attn_fwd(query, keys, values, mask, w_out):
    tokens, width = query.shape
    model = w_out.shape[2]

    def kernel(wo, q, k, v, m, *rest):
        attn_fwd_kernel(q, k, v, m, wo, *rest)

    return call(
        kernel,
        [((tokens // 2, model), F32), ((tokens // 2, model), BF16)],
        [],
        [w_out],
        [query, keys, values, mask],
        [
            pltpu.VMEM((width, model), BF16),
            pltpu.VMEM((tokens, width), BF16),
            pltpu.SemaphoreType.DMA((width // HEAD_DIM,)),
        ],
        2 * tokens * width * model,
    )


def grad_mixing(pieces, w_out):
    tokens = 8 * pieces[0].shape[0]
    width, model = w_out.shape[1:]
    return call(
        grad_mixed_kernel,
        [((tokens, width), BF16)],
        pieces,
        [w_out],
        [],
        [
            pltpu.VMEM((tokens, model), BF16),
            pltpu.VMEM((width, model), BF16),
            pltpu.SemaphoreType.DMA((8,)),
            pltpu.SemaphoreType.DMA((width // HEAD_DIM,)),
        ],
        2 * tokens * width * model,
    )[0]


def attn_bwd(query, keys, values, grad_mixed, mask, cosine, sine):
    tokens, width = query.shape
    return call(
        attn_bwd_kernel,
        [((tokens, width), BF16), ((tokens, HEAD_DIM), BF16), ((tokens, HEAD_DIM), BF16)],
        [],
        [],
        [query, keys, values, grad_mixed, mask, cosine, sine],
        [],
        16 * tokens * tokens * width,
    )


def norm_back(grad_normed, unit, scale, gain, upstream):
    weighted = grad_normed * gain
    inner = jnp.mean(weighted * unit, axis=-1, keepdims=True)
    return (upstream.astype(F32) + scale * (weighted - unit * inner)).astype(BF16)


def back_project(grads, weight):
    return jnp.einsum("tq,dq->td", grads, weight, preferred_element_type=F32)


def body(x_fwd, grad_in, stash, norm_gain, w_query, w_keyval, w_out, slot_table):
    section_idx = lax.axis_index("section")
    sections = lax.axis_size("section")
    is_early = section_idx < sections // 2
    rows = x_fwd.shape[1]
    gain = norm_gain[0]
    weight_q = w_query[0]
    weight_k = w_keyval[0, 0]
    weight_v = w_keyval[0, 1]
    held = stash[0]

    def start_gather(block, tag):
        with jax.named_scope(tag + "_far"):
            far = chip_swap(block, 2)
        with jax.named_scope(tag + "_near"):
            near = chip_swap(block, 1)
        return block, near, far

    def pass_on(far, tag):
        with jax.named_scope(tag + "_last"):
            return chip_swap(far, 1)

    def swap(value, tag):
        with jax.named_scope(tag + "_swap"):
            return core_swap(value)

    own2, near2, far2 = start_gather(grad_in[0], "g2")
    with jax.named_scope("norm_fwd"):
        normed_fwd, _, _ = normalize(x_fwd[0], gain)
    own1, near1, far1 = start_gather(normed_fwd, "g1")
    with jax.named_scope("payload"):
        returned = lax.dynamic_index_in_dim(held, slot_table[0, 0], 0, keepdims=False)
        payload = jnp.where(is_early, x_fwd[0], returned)
        received = lax.ppermute(
            after(payload, normed_fwd), "section", [(i, sections - 1 - i) for i in range(sections)]
        )
    last1 = pass_on(far1, "g1")
    last2 = pass_on(after(far2, far1), "g2")
    mine1 = [own1, near1, far1, last1]
    mine2 = [own2, near2, far2, last2]

    with jax.named_scope("tables"):
        position = local_positions(rows)
        mask = (position[:, None] >= position[None, :]).astype(F32)
        cosine, sine = rope_tables(position, HEAD_DIM)
        cosine, sine = jnp.concatenate([cosine, cosine], axis=1), jnp.concatenate([-sine, sine], axis=1)

    with jax.named_scope("norm_bwd"):
        received = after(received, near1, near2, last1, last2)
        own_block = lax.dynamic_index_in_dim(held, slot_table[0, 1], 0, keepdims=False)
        checkpoint = jnp.where(is_early, received, own_block)
        normed_bwd, unit, scale = normalize(checkpoint, gain)
    own3, near3, far3 = start_gather(normed_bwd, "g3")

    with jax.named_scope("qkv_fwd"):
        pieces = mine1 + [swap(piece, "g1") for piece in mine1]
        pieces = [after(pieces[0], normed_bwd)] + pieces[1:]
        query, keys, values = qkv(pieces, w_query, w_keyval, cosine, sine)
    with jax.named_scope("attn_fwd"):
        part_own, part_other = attn_fwd(query, keys, values, mask, w_out)
    with jax.named_scope("r1_swap"):
        part_other = after(part_other, near3, far3)
        swapped1 = core_swap(part_other)
    last3 = pass_on(after(far3, part_other), "g3")
    mine3 = [own3, near3, far3, last3]
    with jax.named_scope("grad_mixed"):
        pieces = mine2 + [swap(piece, "g2") for piece in mine2]
        pieces = [after(pieces[0], part_other)] + pieces[1:]
        grad_mixed = grad_mixing(pieces, w_out)
    kept1, near1_sum, far1_sum, pass1 = scatter_parts(part_own, swapped1)
    with jax.named_scope("r1_pass"):
        from_near1 = chip_swap(pass1.astype(BF16), 1)
    from_near1 = after(from_near1, last3)
    with jax.named_scope("r1_far"):
        sum_far1 = chip_swap((far1_sum + from_near1.astype(F32)).astype(BF16), 2)
    with jax.named_scope("r1_near"):
        sum_near1 = chip_swap(after(near1_sum, from_near1).astype(BF16), 1)

    with jax.named_scope("qkv_bwd"):
        pieces = mine3 + [swap(piece, "g3") for piece in mine3]
        pieces = [after(pieces[0], from_near1)] + pieces[1:]
        query_b, keys_b, values_b = qkv(pieces, w_query, w_keyval, cosine, sine)
    with jax.named_scope("attn_bwd"):
        grads = attn_bwd(query_b, keys_b, values_b, grad_mixed, mask, cosine, sine)

    with jax.named_scope("fwd_out"):
        attn_part = kept1 + after(sum_near1, grads[0]).astype(F32) + after(sum_far1, grads[0]).astype(F32)
        output = (x_fwd[0].astype(F32) + attn_part).astype(BF16)
        fwd_out = shifted(output[None], 1)
    grads = lax.optimization_barrier((output, *grads))[1:]

    half = 4 * rows

    def grad_rows(low, high):
        total = back_project(grads[0][low:high], weight_q)
        total = total + back_project(grads[1][low:high], weight_k)
        return total + back_project(grads[2][low:high], weight_v)

    with jax.named_scope("back_other"):
        back_other = grad_rows(half, 2 * half).astype(BF16)
    with jax.named_scope("back_own"):
        back_own = grad_rows(0, half)
    with jax.named_scope("r2_swap"):
        swapped2 = core_swap(back_other)
    kept2, near2_sum, far2_sum, pass2 = scatter_parts(back_own, swapped2)
    with jax.named_scope("r2_pass"):
        from_near2 = chip_swap(pass2.astype(BF16), 1)
    with jax.named_scope("r2_far"):
        sum_far2 = chip_swap((far2_sum + from_near2.astype(F32)).astype(BF16), 2)
    with jax.named_scope("r2_near"):
        sum_near2 = chip_swap(after(near2_sum, from_near2).astype(BF16), 1)

    with jax.named_scope("stash_out"):
        slot_ids = jnp.arange(held.shape[0], dtype=jnp.int32)
        replace = jnp.logical_and(slot_ids == slot_table[0, 0], jnp.logical_not(is_early))
        stash_out = jnp.where(replace[:, None, None], received[None], held)[None]
    with jax.named_scope("bwd_out"):
        grad_normed = kept2 + sum_near2.astype(F32) + sum_far2.astype(F32)
        grad_x = norm_back(grad_normed, unit, scale, gain, grad_in[0])
        bwd_out = shifted(grad_x[None], -1)
    return (fwd_out, bwd_out, stash_out)


def solution(mesh):
    placed = (
        P("section", "tensor", None),
        P("section", "tensor", None),
        P("section", None, "tensor", None),
        P("section", None),
        P("section", None, "tensor"),
        P("section", None, None, "tensor"),
        P("section", "tensor", None),
        P("section", None),
    )
    return jax.shard_map(
        body,
        mesh=mesh,
        in_specs=placed,
        out_specs=(
            P("section", "tensor", None),
            P("section", "tensor", None),
            P("section", None, "tensor", None),
        ),
        check_vma=False,
    )
```

time: 308 us -> 160 us (0.52)
  the two profiles are of different devices: /device:TPU:193 before, /device:TPU:62 now
where the time goes in v1:
time: 160 us; the launch traced here: 156 us
  waiting for transfers between devices  74.2 us (46%)
  starting transfers between devices  38.5 us (24%)
  Pallas kernels  16.3 us (10%)
  other arithmetic  12.2 us (8%)
  local copies, waits for them, and re-layouts  5.8 us (4%)
  matrix products  4.69 us (3%)
  between operations  4.62 us (3%)
    ppermute x15, waiting for transfers between devices, chip_swap(): lax.ppermute(value, 'tensor', [(i, i ^ 2 * mask) for i in range(size)])  47.5 us
    ppermute x15, starting transfers between devices, chip_swap(): lax.ppermute(value, 'tensor', [(i, i ^ 2 * mask) for i in range(size)])  21.5 us
    pallas_call x5, Pallas kernels, call(): pl.pallas_call(kernel, out_shape=[jax.ShapeDtypeStruct(shape, dtype) for...  16.3 us
    ppermute x2, waiting for transfers between devices, shifted(): lax.ppermute(value, 'section', [(i, i + steps) for i in range(count) if 0...  12.6 us
    ppermute x1, waiting for transfers between devices, body(): lax.ppermute(after(payload, normed_fwd), 'section', [(i, sections - 1 - i...  10.9 us
    ppermute x2, starting transfers between devices, shifted(): lax.ppermute(value, 'section', [(i, i + steps) for i in range(count) if 0...  8.72 us
    ppermute x1, starting transfers between devices, body(): lax.ppermute(after(payload, normed_fwd), 'section', [(i, sections - 1 - i...  5.42 us
    dot_general x6, matrix products, back_project(): return jnp.einsum('tq,dq->td', grads, weight, preferred_element_type=F32)  4.69 us
  transfers between devices with their start and end apart: 32, of which 15 were waited for; matrix products, arithmetic and copies ran while one was open for 9% of the time, Pallas kernels for 10%

profile of v1, /device:TPU:62, one launch (start us, length us, event | category | flops | bytes accessed | tf_op | source)
XLA Modules:
  0.0 156.4 jit_solution(2207681481655705234)
XLA Ops:
  3.0 3.4 %collective-permute-start.3 = (bf16[32,4096]{1,0:T(8,128)(2,1)S(1)}, bf16[32,4096]{1,0:T(8,128)(2,1)S(1)}, u32[]{:S(2)}, u32[]{:S(2)}) collective-permute-start(bf16[32,4096]{1,0:T(8,128)(2,1)S(1)} %fusion.25.refs_0_), channel_id=1, source_target_pairs={{0,4},{1,5},{2,6},{3,7},{4,0},{5,1},{6,2},{7,3},{8,12},{9,13},{10,... | collective-permute-start | bytes 786440 | tf_op jit(solution)/shard_map/g1_far/ppermute | solution.py:23
  6.6 1.9 %collective-permute-start.2 = (bf16[32,4096]{1,0:T(8,128)(2,1)}, bf16[32,4096]{1,0:T(8,128)(2,1)S(1)}, u32[]{:S(2)}, u32[]{:S(2)}) collective-permute-start(bf16[32,4096]{1,0:T(8,128)(2,1)} %bitcast.42), channel_id=1, source_target_pairs={{0,2},{1,3},{2,0},{3,1},{4,6},{5,7},{6,4},{7,5},{8,10},{9,11},{10,... | collective-permute-start | bytes 786440 | tf_op jit(solution)/shard_map/g2_near/ppermute | solution.py:23
  13.5 5.4 %collective-permute-start = (bf16[32,4096]{1,0:T(8,128)(2,1)}, bf16[32,4096]{1,0:T(8,128)(2,1)}, u32[]{:S(2)}, u32[]{:S(2)}) collective-permute-start(bf16[32,4096]{1,0:T(8,128)(2,1)} %bitcast_select_fusion.1), channel_id=1, source_target_pairs={{0,248},{8,240},{16,232},{24,224},{32,216},{40,208},{48,200},{56,1... | collective-permute-start | bytes 786440 | tf_op jit(solution)/shard_map/payload/ppermute | solution.py:323
  19.0 11.6 %collective-permute-done.5.refs_2_ = bf16[32,4096]{1,0:T(8,128)(2,1)S(1)} collective-permute-done((bf16[32,4096]{1,0:T(8,128)(2,1)}, bf16[32,4096]{1,0:T(8,128)(2,1)S(1)}, u32[]{:S(2)}, u32[]{:S(2)}) %collective-permute-start.5) | collective-permute-done | bytes 262176 | tf_op jit(solution)/shard_map/g2_far/ppermute | solution.py:23
  30.6 2.0 %collective-permute-start.4 = (bf16[32,4096]{1,0:T(8,128)(2,1)S(1)}, bf16[32,4096]{1,0:T(8,128)(2,1)}, u32[]{:S(2)}, u32[]{:S(2)}) collective-permute-start(bf16[32,4096]{1,0:T(8,128)(2,1)S(1)} %collective-permute-done.3.refs_2_), channel_id=1, source_target_pairs={{0,2},{1,3},{2,0},{3,1},{4,6},{5,7},{6,4},{7,5},{8,10},{9,11},{10,... | collective-permute-start | bytes 786440 | tf_op jit(solution)/shard_map/g1_last/ppermute | solution.py:23
  35.0 10.9 %collective-permute-done = bf16[32,4096]{1,0:T(8,128)(2,1)} collective-permute-done((bf16[32,4096]{1,0:T(8,128)(2,1)}, bf16[32,4096]{1,0:T(8,128)(2,1)}, u32[]{:S(2)}, u32[]{:S(2)}) %collective-permute-start) | collective-permute-done | bytes 262176 | tf_op jit(solution)/shard_map/payload/ppermute | solution.py:323
  47.4 4.6 %collective-permute-done.4.refs_3_ = bf16[32,4096]{1,0:T(8,128)(2,1)} collective-permute-done((bf16[32,4096]{1,0:T(8,128)(2,1)S(1)}, bf16[32,4096]{1,0:T(8,128)(2,1)}, u32[]{:S(2)}, u32[]{:S(2)}) %collective-permute-start.4) | collective-permute-done | bytes 262176 | tf_op jit(solution)/shard_map/g1_last/ppermute | solution.py:23
  54.1 2.0 %collective-permute-start.12 = (bf16[32,4096]{1,0:T(8,128)(2,1)S(1)}, bf16[32,4096]{1,0:T(8,128)(2,1)S(1)}, u32[]{:S(2)}, u32[]{:S(2)}) collective-permute-start(bf16[32,4096]{1,0:T(8,128)(2,1)S(1)} %fusion.16.refs_0_), channel_id=1, source_target_pairs={{0,4},{1,5},{2,6},{3,7},{4,0},{5,1},{6,2},{7,3},{8,12},{9,13},{10,... | collective-permute-start | bytes 786440 | tf_op jit(solution)/shard_map/g3_far/ppermute | solution.py:23
  58.1 2.2 %copy-done = bf16[1,4096,512]{2,1,0:T(8,128)(2,1)S(1)} copy-done((bf16[1,4096,512]{2,1,0:T(8,128)(2,1)S(1)}, bf16[1,4096,512]{2,1,0:T(8,128)(2,1)}, u32[]{:S(2)}) %copy-start) | copy-done | bytes 4194328
  60.3 4.3 %qkv_fwd.1 = (bf16[256,512]{1,0:T(8,128)(2,1)S(1)}, bf16[256,128]{1,0:T(8,128)(2,1)S(1)}, bf16[256,128]{1,0:T(8,128)(2,1)S(1)}) custom-call(bf16[32,4096]{1,0:T(8,128)(2,1)S(1)} %fusion.25.refs_0_, bf16[32,4096]{1,0:T(8,128)(2,1)} %collective-permute-done.1.refs_1_, bf16[32,4096]{1,0:T(8,128)(2,1)S(1)} %collective-permute-done.3.refs_2_, ...), custom_call_target="tpu_custom_call" | custom-call | flops 25165824 | bytes 65536 | tf_op jit(solution)/shard_map/qkv_fwd/pallas_call | solution.py:194
  64.6 2.7 %attn_fwd.1 = (f32[128,4096]{1,0:T(8,128)S(1)}, bf16[128,4096]{1,0:T(8,128)(2,1)S(1)}) custom-call(bf16[1,512,4096]{2,1,0:T(8,128)(2,1)S(1)} %copy-done.3, bf16[256,512]{1,0:T(8,128)(2,1)S(1)} %get-tuple-element.34.q, bf16[256,128]{1,0:T(8,128)(2,1)S(1)} %get-tuple-element.35.k, bf16[256,128]{1,0:T(8,128)(2,1)S(1)} %get-tuple-element.36.v, ...), custom_call_target="tpu_custom_call" | custom-call | flops 16777216 | bytes 65536 | tf_op jit(solution)/shard_map/attn_fwd/pallas_call | solution.py:194
  72.0 6.6 %collective-permute-done.15.refs_3_ = bf16[32,4096]{1,0:T(8,128)(2,1)S(1)} collective-permute-done((bf16[32,4096]{1,0:T(8,128)(2,1)S(1)}, bf16[32,4096]{1,0:T(8,128)(2,1)S(1)}, u32[]{:S(2)}, u32[]{:S(2)}) %collective-permute-start.15) | collective-permute-done | bytes 262176 | tf_op jit(solution)/shard_map/g3_last/ppermute | solution.py:23
  80.3 5.7 %collective-permute-done.14 = bf16[32,4096]{1,0:T(8,128)(2,1)S(1)} collective-permute-done((bf16[32,4096]{1,0:T(8,128)(2,1)S(1)}, bf16[32,4096]{1,0:T(8,128)(2,1)S(1)}, u32[]{:S(2)}, u32[]{:S(2)}) %collective-permute-start.14) | collective-permute-done | bytes 262176 | tf_op jit(solution)/shard_map/r1_pass/ppermute | solution.py:23
  90.2 3.1 %grad_mixed.1.gm = bf16[256,512]{1,0:T(8,128)(2,1)S(1)} custom-call(bf16[32,4096]{1,0:T(8,128)(2,1)S(1)} %bitcast.44, bf16[32,4096]{1,0:T(8,128)(2,1)S(1)} %collective-permute-done.2.refs_1_, bf16[32,4096]{1,0:T(8,128)(2,1)S(1)} %collective-permute-done.5.refs_2_, bf16[32,4096]{1,0:T(8,128)(2,1)S(1)} %collective-permute-done.6.refs_3_, ...), custom_call_target="tpu_custom_call" | custom-call | flops 16777216 | bytes 65536 | tf_op jit(solution)/shard_map/grad_mixed/pallas_call | solution.py:194
  93.4 3.9 %qkv_bwd.1 = (bf16[256,512]{1,0:T(8,128)(2,1)S(1)}, bf16[256,128]{1,0:T(8,128)(2,1)S(1)}, bf16[256,128]{1,0:T(8,128)(2,1)S(1)}) custom-call(bf16[32,4096]{1,0:T(8,128)(2,1)S(1)} %fusion.16.refs_0_, bf16[32,4096]{1,0:T(8,128)(2,1)S(1)} %collective-permute-done.11.refs_1_, bf16[32,4096]{1,0:T(8,128)(2,1)S(1)} %collective-permute-done.12.refs_2_, ...), custom_call_target="tpu_custom_call" | custom-call | flops 25165824 | bytes 65536 | tf_op jit(solution)/shard_map/qkv_bwd/pallas_call | solution.py:194
  97.3 2.3 %attn_bwd.1 = (bf16[256,512]{1,0:T(8,128)(2,1)S(1)}, bf16[256,128]{1,0:T(8,128)(2,1)S(1)}, bf16[256,128]{1,0:T(8,128)(2,1)S(1)}) custom-call(bf16[256,512]{1,0:T(8,128)(2,1)S(1)} %get-tuple-element.44.q, bf16[256,128]{1,0:T(8,128)(2,1)S(1)} %get-tuple-element.45.k, bf16[256,128]{1,0:T(8,128)(2,1)S(1)} %get-tuple-element.46.v, ...), custom_call_target="tpu_custom_call" | custom-call | flops 8388608 | bytes 65536 | tf_op jit(solution)/shard_map/attn_bwd/pallas_call | solution.py:194
  99.6 2.2 %collective-permute-done.25 = bf16[32,4096]{1,0:T(8,128)(2,1)S(1)} collective-permute-done((bf16[32,4096]{1,0:T(8,128)(2,1)S(1)}, bf16[32,4096]{1,0:T(8,128)(2,1)S(1)}, u32[]{:S(2)}, u32[]{:S(2)}) %collective-permute-start.25) | collective-permute-done | bytes 262176 | tf_op jit(solution)/shard_map/r1_far/ppermute | solution.py:23
  107.1 2.5 %collective-permute-start.28 = (bf16[32,4096]{1,0:T(8,128)(2,1)S(1)}, bf16[32,4096]{1,0:T(8,128)(2,1)S(1)}, u32[]{:S(2)}, u32[]{:S(2)}) collective-permute-start(bf16[32,4096]{1,0:T(8,128)(2,1)S(1)} %fusion.29), channel_id=1, source_target_pairs={{0,2},{1,3},{2,0},{3,1},{4,6},{5,7},{6,4},{7,5},{8,10},{9,11},{10,... | collective-permute-start | bytes 786440 | tf_op jit(solution)/shard_map/r2_pass/ppermute | solution.py:23
  109.7 6.7 %collective-permute-done.28 = bf16[32,4096]{1,0:T(8,128)(2,1)S(1)} collective-permute-done((bf16[32,4096]{1,0:T(8,128)(2,1)S(1)}, bf16[32,4096]{1,0:T(8,128)(2,1)S(1)}, u32[]{:S(2)}, u32[]{:S(2)}) %collective-permute-start.28) | collective-permute-done | bytes 262176 | tf_op jit(solution)/shard_map/r2_pass/ppermute | solution.py:23
  119.8 6.8 %collective-permute-start.26 = (bf16[1,32,4096]{2,1,0:T(8,128)(2,1)S(1)}, bf16[1,32,4096]{2,1,0:T(8,128)(2,1)S(1)}, u32[]{:S(2)}, u32[]{:S(2)}) collective-permute-start(bf16[1,32,4096]{2,1,0:T(8,128)(2,1)S(1)} %bitcast.49), channel_id=1, source_target_pairs={{0,8},{8,16},{16,24},{24,32},{32,40},{40,48},{48,56},{56,64},{64,7... | collective-permute-start | bytes 786440 | tf_op jit(solution)/shard_map/fwd_out/ppermute | solution.py:28
  126.6 3.9 %collective-permute-done.29 = bf16[32,4096]{1,0:T(8,128)(2,1)S(1)} collective-permute-done((bf16[32,4096]{1,0:T(8,128)(2,1)S(1)}, bf16[32,4096]{1,0:T(8,128)(2,1)S(1)}, u32[]{:S(2)}, u32[]{:S(2)}) %collective-permute-start.29) | collective-permute-done | bytes 262176 | tf_op jit(solution)/shard_map/r2_near/ppermute | solution.py:23
  130.6 5.2 %collective-permute-done.30 = bf16[32,4096]{1,0:T(8,128)(2,1)S(1)} collective-permute-done((bf16[32,4096]{1,0:T(8,128)(2,1)S(1)}, bf16[32,4096]{1,0:T(8,128)(2,1)S(1)}, u32[]{:S(2)}, u32[]{:S(2)}) %collective-permute-start.30) | collective-permute-done | bytes 262176 | tf_op jit(solution)/shard_map/r2_far/ppermute | solution.py:23
  138.6 1.9 %collective-permute-start.31 = (bf16[1,32,4096]{2,1,0:T(8,128)(2,1)S(1)}, bf16[1,32,4096]{2,1,0:T(8,128)(2,1)S(1)}, u32[]{:S(2)}, u32[]{:S(2)}) collective-permute-start(bf16[1,32,4096]{2,1,0:T(8,128)(2,1)S(1)} %fusion.33), channel_id=1, source_target_pairs={{8,0},{16,8},{24,16},{32,24},{40,32},{48,40},{56,48},{64,56},{72,6... | collective-permute-start | bytes 786440 | tf_op jit(solution)/shard_map/bwd_out/ppermute | solution.py:28
  142.4 12.6 %collective-permute-done.31 = bf16[1,32,4096]{2,1,0:T(8,128)(2,1)S(1)} collective-permute-done((bf16[1,32,4096]{2,1,0:T(8,128)(2,1)S(1)}, bf16[1,32,4096]{2,1,0:T(8,128)(2,1)S(1)}, u32[]{:S(2)}, u32[]{:S(2)}) %collective-permute-start.31) | collective-permute-done | bytes 262176 | tf_op jit(solution)/shard_map/bwd_out/ppermute | solution.py:28
  (106 shorter events, 37.5 us)
Async XLA Ops:
  3.0 16.0 %collective-permute-start.3 = (bf16[32,4096]{1,0:T(8,128)(2,1)S(1)}, bf16[32,4096]{1,0:T(8,128)(2,1)S(1)}, u32[]{:S(2)}, u32[]{:S(2)}) collective-permute-start(bf16[32,4096]{1,0:T(8,128)(2,1)S(1)} %fusion.25.refs_0_), channel_id=1, source_target_pairs={{0,4},{1,5},{2,6},{3,7},{4,0},{5,1},{6,2},{7,3},{8,12},{9,13},{10,... | collective-permute-start | bytes 786440 | tf_op jit(solution)/shard_map/g1_far/ppermute | solution.py:23
  6.4 39.5 %collective-permute-start.1 = (bf16[32,4096]{1,0:T(8,128)(2,1)S(1)}, bf16[32,4096]{1,0:T(8,128)(2,1)}, u32[]{:S(2)}, u32[]{:S(2)}) collective-permute-start(bf16[32,4096]{1,0:T(8,128)(2,1)S(1)} %fusion.25.refs_0_), channel_id=1, source_target_pairs={{0,2},{1,3},{2,0},{3,1},{4,6},{5,7},{6,4},{7,5},{8,10},{9,11},{10,... | collective-permute-start | bytes 786440 | tf_op jit(solution)/shard_map/g1_near/ppermute | solution.py:23
  6.5 24.1 %collective-permute-start.5 = (bf16[32,4096]{1,0:T(8,128)(2,1)}, bf16[32,4096]{1,0:T(8,128)(2,1)S(1)}, u32[]{:S(2)}, u32[]{:S(2)}) collective-permute-start(bf16[32,4096]{1,0:T(8,128)(2,1)} %bitcast.41), channel_id=1, source_target_pairs={{0,4},{1,5},{2,6},{3,7},{4,0},{5,1},{6,2},{7,3},{8,12},{9,13},{10,... | collective-permute-start | bytes 786440 | tf_op jit(solution)/shard_map/g2_far/ppermute | solution.py:23
  6.6 39.8 %collective-permute-start.2 = (bf16[32,4096]{1,0:T(8,128)(2,1)}, bf16[32,4096]{1,0:T(8,128)(2,1)S(1)}, u32[]{:S(2)}, u32[]{:S(2)}) collective-permute-start(bf16[32,4096]{1,0:T(8,128)(2,1)} %bitcast.42), channel_id=1, source_target_pairs={{0,2},{1,3},{2,0},{3,1},{4,6},{5,7},{6,4},{7,5},{8,10},{9,11},{10,... | collective-permute-start | bytes 786440 | tf_op jit(solution)/shard_map/g2_near/ppermute | solution.py:23
  13.5 32.4 %collective-permute-start = (bf16[32,4096]{1,0:T(8,128)(2,1)}, bf16[32,4096]{1,0:T(8,128)(2,1)}, u32[]{:S(2)}, u32[]{:S(2)}) collective-permute-start(bf16[32,4096]{1,0:T(8,128)(2,1)} %bitcast_select_fusion.1), channel_id=1, source_target_pairs={{0,248},{8,240},{16,232},{24,224},{32,216},{40,208},{48,200},{56,1... | collective-permute-start | bytes 786440 | tf_op jit(solution)/shard_map/payload/ppermute | solution.py:323
  30.6 16.8 %collective-permute-start.6 = (bf16[32,4096]{1,0:T(8,128)(2,1)S(1)}, bf16[32,4096]{1,0:T(8,128)(2,1)S(1)}, u32[]{:S(2)}, u32[]{:S(2)}) collective-permute-start(bf16[32,4096]{1,0:T(8,128)(2,1)S(1)} %collective-permute-done.5.refs_2_), channel_id=1, source_target_pairs={{0,2},{1,3},{2,0},{3,1},{4,6},{5,7},{6,4},{7,5},{8,10},{9,11},{10,... | collective-permute-start | bytes 786440 | tf_op jit(solution)/shard_map/g2_last/ppermute | solution.py:23
  30.6 21.4 %collective-permute-start.4 = (bf16[32,4096]{1,0:T(8,128)(2,1)S(1)}, bf16[32,4096]{1,0:T(8,128)(2,1)}, u32[]{:S(2)}, u32[]{:S(2)}) collective-permute-start(bf16[32,4096]{1,0:T(8,128)(2,1)S(1)} %collective-permute-done.3.refs_2_), channel_id=1, source_target_pairs={{0,2},{1,3},{2,0},{3,1},{4,6},{5,7},{6,4},{7,5},{8,10},{9,11},{10,... | collective-permute-start | bytes 786440 | tf_op jit(solution)/shard_map/g1_last/ppermute | solution.py:23
  45.8 10.5 %collective-permute-start.7 = (bf16[32,4096]{1,0:T(8,128)(2,1)S(1)}, bf16[32,4096]{1,0:T(8,128)(2,1)S(1)}, u32[]{:S(2)}, u32[]{:S(2)}) collective-permute-start(bf16[32,4096]{1,0:T(8,128)(2,1)S(1)} %fusion.25.refs_0_), channel_id=1, source_target_pairs={{0,1},{1,0},{2,3},{3,2},{4,5},{5,4},{6,7},{7,6},{8,9},{9,8},{10,11... | collective-permute-start | bytes 786440 | tf_op jit(solution)/shard_map/qkv_fwd/g1_swap/ppermute | solution.py:18
  45.8 10.8 %collective-permute-start.9 = (bf16[32,4096]{1,0:T(8,128)(2,1)S(1)}, bf16[32,4096]{1,0:T(8,128)(2,1)S(1)}, u32[]{:S(2)}, u32[]{:S(2)}) collective-permute-start(bf16[32,4096]{1,0:T(8,128)(2,1)S(1)} %collective-permute-done.3.refs_2_), channel_id=1, source_target_pairs={{0,1},{1,0},{2,3},{3,2},{4,5},{5,4},{6,7},{7,6},{8,9},{9,8},{10,11... | collective-permute-start | bytes 786440 | tf_op jit(solution)/shard_map/qkv_fwd/g1_swap/ppermute | solution.py:18
  46.4 10.3 %collective-permute-start.8 = (bf16[32,4096]{1,0:T(8,128)(2,1)}, bf16[32,4096]{1,0:T(8,128)(2,1)S(1)}, u32[]{:S(2)}, u32[]{:S(2)}) collective-permute-start(bf16[32,4096]{1,0:T(8,128)(2,1)} %collective-permute-done.1.refs_1_), channel_id=1, source_target_pairs={{0,1},{1,0},{2,3},{3,2},{4,5},{5,4},{6,7},{7,6},{8,9},{9,8},{10,11... | collective-permute-start | bytes 786440 | tf_op jit(solution)/shard_map/qkv_fwd/g1_swap/ppermute | solution.py:18
  54.1 13.3 %collective-permute-start.12 = (bf16[32,4096]{1,0:T(8,128)(2,1)S(1)}, bf16[32,4096]{1,0:T(8,128)(2,1)S(1)}, u32[]{:S(2)}, u32[]{:S(2)}) collective-permute-start(bf16[32,4096]{1,0:T(8,128)(2,1)S(1)} %fusion.16.refs_0_), channel_id=1, source_target_pairs={{0,4},{1,5},{2,6},{3,7},{4,0},{5,1},{6,2},{7,3},{8,12},{9,13},{10,... | collective-permute-start | bytes 786440 | tf_op jit(solution)/shard_map/g3_far/ppermute | solution.py:23
  56.1 11.4 %collective-permute-start.11 = (bf16[32,4096]{1,0:T(8,128)(2,1)S(1)}, bf16[32,4096]{1,0:T(8,128)(2,1)S(1)}, u32[]{:S(2)}, u32[]{:S(2)}) collective-permute-start(bf16[32,4096]{1,0:T(8,128)(2,1)S(1)} %fusion.16.refs_0_), channel_id=1, source_target_pairs={{0,2},{1,3},{2,0},{3,1},{4,6},{5,7},{6,4},{7,5},{8,10},{9,11},{10,... | collective-permute-start | bytes 786440 | tf_op jit(solution)/shard_map/g3_near/ppermute | solution.py:23
  67.6 18.4 %collective-permute-start.21 = (bf16[32,4096]{1,0:T(8,128)(2,1)S(1)}, bf16[32,4096]{1,0:T(8,128)(2,1)S(1)}, u32[]{:S(2)}, u32[]{:S(2)}) collective-permute-start(bf16[32,4096]{1,0:T(8,128)(2,1)S(1)} %bitcast.43), channel_id=1, source_target_pairs={{0,1},{1,0},{2,3},{3,2},{4,5},{5,4},{6,7},{7,6},{8,9},{9,8},{10,11... | collective-permute-start | bytes 786440 | tf_op jit(solution)/shard_map/grad_mixed/g2_swap/ppermute | solution.py:18
  68.0 18.5 %collective-permute-start.22 = (bf16[32,4096]{1,0:T(8,128)(2,1)S(1)}, bf16[32,4096]{1,0:T(8,128)(2,1)S(1)}, u32[]{:S(2)}, u32[]{:S(2)}) collective-permute-start(bf16[32,4096]{1,0:T(8,128)(2,1)S(1)} %collective-permute-done.2.refs_1_), channel_id=1, source_target_pairs={{0,1},{1,0},{2,3},{3,2},{4,5},{5,4},{6,7},{7,6},{8,9},{9,8},{10,11... | collective-permute-start | bytes 786440 | tf_op jit(solution)/shard_map/grad_mixed/g2_swap/ppermute | solution.py:18
  68.2 18.5 %collective-permute-start.23 = (bf16[32,4096]{1,0:T(8,128)(2,1)S(1)}, bf16[32,4096]{1,0:T(8,128)(2,1)S(1)}, u32[]{:S(2)}, u32[]{:S(2)}) collective-permute-start(bf16[32,4096]{1,0:T(8,128)(2,1)S(1)} %collective-permute-done.5.refs_2_), channel_id=1, source_target_pairs={{0,1},{1,0},{2,3},{3,2},{4,5},{5,4},{6,7},{7,6},{8,9},{9,8},{10,11... | collective-permute-start | bytes 786440 | tf_op jit(solution)/shard_map/grad_mixed/g2_swap/ppermute | solution.py:18
  68.5 18.5 %collective-permute-start.24 = (bf16[32,4096]{1,0:T(8,128)(2,1)S(1)}, bf16[32,4096]{1,0:T(8,128)(2,1)S(1)}, u32[]{:S(2)}, u32[]{:S(2)}) collective-permute-start(bf16[32,4096]{1,0:T(8,128)(2,1)S(1)} %collective-permute-done.6.refs_3_), channel_id=1, source_target_pairs={{0,1},{1,0},{2,3},{3,2},{4,5},{5,4},{6,7},{7,6},{8,9},{9,8},{10,11... | collective-permute-start | bytes 786440 | tf_op jit(solution)/shard_map/grad_mixed/g2_swap/ppermute | solution.py:18
  70.2 8.3 %collective-permute-start.15 = (bf16[32,4096]{1,0:T(8,128)(2,1)S(1)}, bf16[32,4096]{1,0:T(8,128)(2,1)S(1)}, u32[]{:S(2)}, u32[]{:S(2)}) collective-permute-start(bf16[32,4096]{1,0:T(8,128)(2,1)S(1)} %collective-permute-done.12.refs_2_), channel_id=1, source_target_pairs={{0,2},{1,3},{2,0},{3,1},{4,6},{5,7},{6,4},{7,5},{8,10},{9,11},{10,... | collective-permute-start | bytes 786440 | tf_op jit(solution)/shard_map/g3_last/ppermute | solution.py:23
  87.1 12.5 %collective-permute-start.16 = (bf16[32,4096]{1,0:T(8,128)(2,1)S(1)}, bf16[32,4096]{1,0:T(8,128)(2,1)S(1)}, u32[]{:S(2)}, u32[]{:S(2)}) collective-permute-start(bf16[32,4096]{1,0:T(8,128)(2,1)S(1)} %convert_add_fusion.1), channel_id=1, source_target_pairs={{0,2},{1,3},{2,0},{3,1},{4,6},{5,7},{6,4},{7,5},{8,10},{9,11},{10,... | collective-permute-start | bytes 786440 | tf_op jit(solution)/shard_map/r1_near/ppermute | solution.py:23
  88.9 12.9 %collective-permute-start.25 = (bf16[32,4096]{1,0:T(8,128)(2,1)S(1)}, bf16[32,4096]{1,0:T(8,128)(2,1)S(1)}, u32[]{:S(2)}, u32[]{:S(2)}) collective-permute-start(bf16[32,4096]{1,0:T(8,128)(2,1)S(1)} %add_convert_fusion), channel_id=1, source_target_pairs={{0,4},{1,5},{2,6},{3,7},{4,0},{5,1},{6,2},{7,3},{8,12},{9,13},{10,... | collective-permute-start | bytes 786440 | tf_op jit(solution)/shard_map/r1_far/ppermute | solution.py:23
  107.1 9.2 %collective-permute-start.28 = (bf16[32,4096]{1,0:T(8,128)(2,1)S(1)}, bf16[32,4096]{1,0:T(8,128)(2,1)S(1)}, u32[]{:S(2)}, u32[]{:S(2)}) collective-permute-start(bf16[32,4096]{1,0:T(8,128)(2,1)S(1)} %fusion.29), channel_id=1, source_target_pairs={{0,2},{1,3},{2,0},{3,1},{4,6},{5,7},{6,4},{7,5},{8,10},{9,11},{10,... | collective-permute-start | bytes 786440 | tf_op jit(solution)/shard_map/r2_pass/ppermute | solution.py:23
  116.4 14.2 %collective-permute-start.29 = (bf16[32,4096]{1,0:T(8,128)(2,1)S(1)}, bf16[32,4096]{1,0:T(8,128)(2,1)S(1)}, u32[]{:S(2)}, u32[]{:S(2)}) collective-permute-start(bf16[32,4096]{1,0:T(8,128)(2,1)S(1)} %slice_add_fusion.2), channel_id=1, source_target_pairs={{0,2},{1,3},{2,0},{3,1},{4,6},{5,7},{6,4},{7,5},{8,10},{9,11},{10,... | collective-permute-start | bytes 786440 | tf_op jit(solution)/shard_map/r2_near/ppermute | solution.py:23
  118.2 17.5 %collective-permute-start.30 = (bf16[32,4096]{1,0:T(8,128)(2,1)S(1)}, bf16[32,4096]{1,0:T(8,128)(2,1)S(1)}, u32[]{:S(2)}, u32[]{:S(2)}) collective-permute-start(bf16[32,4096]{1,0:T(8,128)(2,1)S(1)} %fusion.28), channel_id=1, source_target_pairs={{0,4},{1,5},{2,6},{3,7},{4,0},{5,1},{6,2},{7,3},{8,12},{9,13},{10,... | collective-permute-start | bytes 786440 | tf_op jit(solution)/shard_map/r2_far/ppermute | solution.py:23
  119.8 22.5 %collective-permute-start.26 = (bf16[1,32,4096]{2,1,0:T(8,128)(2,1)S(1)}, bf16[1,32,4096]{2,1,0:T(8,128)(2,1)S(1)}, u32[]{:S(2)}, u32[]{:S(2)}) collective-permute-start(bf16[1,32,4096]{2,1,0:T(8,128)(2,1)S(1)} %bitcast.49), channel_id=1, source_target_pairs={{0,8},{8,16},{16,24},{24,32},{32,40},{40,48},{48,56},{56,64},{64,7... | collective-permute-start | bytes 786440 | tf_op jit(solution)/shard_map/fwd_out/ppermute | solution.py:28
  138.6 16.4 %collective-permute-start.31 = (bf16[1,32,4096]{2,1,0:T(8,128)(2,1)S(1)}, bf16[1,32,4096]{2,1,0:T(8,128)(2,1)S(1)}, u32[]{:S(2)}, u32[]{:S(2)}) collective-permute-start(bf16[1,32,4096]{2,1,0:T(8,128)(2,1)S(1)} %fusion.33), channel_id=1, source_target_pairs={{8,0},{16,8},{24,16},{32,24},{40,32},{48,40},{56,48},{64,56},{72,6... | collective-permute-start | bytes 786440 | tf_op jit(solution)/shard_map/bwd_out/ppermute | solution.py:28
  (20 other events, 244.8 us)

commit v2 on v1

--- a/solution.py
+++ b/solution.py
@@ -9,6 +9,8 @@
 EPS = 1e-05
 THETA = 500000.0
 CHUNKS = 4
+PIECES = 4
+ORDER = (0, 2, 1, 3)
 F32 = jnp.float32
 BF16 = jnp.bfloat16
 
@@ -42,7 +44,7 @@
 
 def local_positions(rows):
     index = lax.axis_index("tensor")
-    blocks = [index ^ (2 * j + k) for k in range(2) for j in range(4)]
+    blocks = [index ^ (2 * j + k) for k in range(2) for j in ORDER]
     start = jnp.stack(blocks) * rows
     return (start[:, None] + jnp.arange(rows, dtype=jnp.int32)[None, :]).reshape(-1)
 
@@ -54,13 +56,6 @@
     return (jnp.cos(angle), jnp.sin(angle))
 
 
-def normalize(block, gain):
-    wide = block.astype(F32)
-    scale = lax.rsqrt(jnp.mean(wide * wide, axis=-1, keepdims=True) + EPS)
-    unit = wide * scale
-    return ((unit * gain).astype(BF16), unit, scale)
-
-
 def swing(values, cosine, sine):
     return values * cosine + pltpu.roll(values, HEAD_DIM // 2, 1) * sine
 
@@ -70,18 +65,19 @@
 
 
 def copy_pieces(pieces, tokens, sems):
-    rows = tokens.shape[0] // len(pieces)
-    copies = [
-        pltpu.make_async_copy(piece, tokens.at[pl.ds(i * rows, rows)], sems.at[i]) for i, piece in enumerate(pieces)
-    ]
-    for copy in copies:
-        copy.start()
+    copies = []
+    low = 0
+    for i, piece in enumerate(pieces):
+        rows = piece.shape[0]
+        copies.append(pltpu.make_async_copy(piece, tokens.at[pl.ds(low, rows)], sems.at[i]))
+        copies[-1].start()
+        low += rows
     return copies
 
 
 def qkv_kernel(*refs):
-    pieces = refs[:8]
-    wq, wkv, cosine, sine, q_out, k_out, v_out, tokens, weights, acc, sems, wsems = refs[8:]
+    pieces = refs[:PIECES]
+    wq, wkv, cosine, sine, q_out, k_out, v_out, tokens, weights, acc, sems, wsems = refs[PIECES:]
     depth = wq.shape[1] // CHUNKS
     width = wq.shape[2]
     copies = copy_pieces(pieces, tokens, sems)
@@ -148,8 +144,8 @@
 
 
 def grad_mixed_kernel(*refs):
-    pieces = refs[:8]
-    wo, out, tokens, weights, sems, wsems = refs[8:]
+    pieces = refs[:PIECES]
+    wo, out, tokens, weights, sems, wsems = refs[PIECES:]
     heads = out.shape[1] // HEAD_DIM
     copies = copy_pieces(pieces, tokens, sems)
     loads = []
@@ -194,16 +190,16 @@
     return pl.pallas_call(
         kernel,
         out_shape=[jax.ShapeDtypeStruct(shape, dtype) for shape, dtype in outs],
-        in_specs=[pl.BlockSpec(memory_space=pl.ANY)] * len(moved) + [pl.BlockSpec(memory_space=pltpu.HBM)] * len(hbm) + [pl.BlockSpec(memory_space=pltpu.VMEM)] * len(vmem),
+        in_specs=[pl.BlockSpec(memory_space=pl.ANY)] * len(moved) + [pl.BlockSpec(memory_space=pl.ANY)] * len(hbm) + [pl.BlockSpec(memory_space=pltpu.VMEM)] * len(vmem),
         out_specs=[pl.BlockSpec(memory_space=pltpu.VMEM)] * len(outs),
         scratch_shapes=scratch,
-        compiler_params=pltpu.CompilerParams(vmem_limit_bytes=40 * 1024 * 1024),
+        compiler_params=pltpu.CompilerParams(vmem_limit_bytes=12 * 1024 * 1024),
         cost_estimate=pl.CostEstimate(flops=flops // 64, bytes_accessed=65536, transcendentals=0),
     )(*moved, *hbm, *vmem)
 
 
 def qkv(pieces, w_query, w_keyval, cosine, sine):
-    tokens = 8 * pieces[0].shape[0]
+    tokens = sum(piece.shape[0] for piece in pieces)
     depth, width = w_query.shape[1:]
     full = width + 2 * HEAD_DIM
     return call(
@@ -216,7 +212,7 @@
             pltpu.VMEM((tokens, depth), BF16),
             pltpu.VMEM((depth, full), BF16),
             pltpu.VMEM((tokens, full), F32),
-            pltpu.SemaphoreType.DMA((8,)),
+            pltpu.SemaphoreType.DMA((PIECES,)),
             pltpu.SemaphoreType.DMA((CHUNKS, 3)),
         ],
         2 * tokens * depth * full,
@@ -246,7 +242,7 @@
 
 
 def grad_mixing(pieces, w_out):
-    tokens = 8 * pieces[0].shape[0]
+    tokens = sum(piece.shape[0] for piece in pieces)
     width, model = w_out.shape[1:]
     return call(
         grad_mixed_kernel,
@@ -257,7 +253,7 @@
         [
             pltpu.VMEM((tokens, model), BF16),
             pltpu.VMEM((width, model), BF16),
-            pltpu.SemaphoreType.DMA((8,)),
+            pltpu.SemaphoreType.DMA((PIECES,)),
             pltpu.SemaphoreType.DMA((width // HEAD_DIM,)),
         ],
         2 * tokens * width * model,
@@ -277,10 +273,59 @@
     )
 
 
-def norm_back(grad_normed, unit, scale, gain, upstream):
-    weighted = grad_normed * gain
+def chosen(slots, column, early, held):
+    block = held[0, 0]
+    for i in range(1, held.shape[1]):
+        block = jnp.where(slots[0, column] == i, held[0, i], block)
+    is_early = lax.axis_index("section") < lax.axis_size("section") // 2
+    return jnp.where(is_early, early, block)
+
+
+def payload_kernel(slots, x, held, out):
+    out[...] = chosen(slots, 0, x[0], held)
+
+
+def checkpoint_kernel(slots, received, held, gain, block_out, normed_out):
+    block = chosen(slots, 1, received[...], held)
+    block_out[...] = block
+    normed_out[...] = (unit_rows(block)[0] * gain[...]).astype(BF16)
+
+
+def with_slots(kernel, outs, slots, *operands):
+    return pl.pallas_call(
+        kernel,
+        out_shape=[jax.ShapeDtypeStruct(shape, BF16) for shape in outs],
+        in_specs=[pl.BlockSpec(memory_space=pltpu.SMEM)] + [pl.BlockSpec(memory_space=pltpu.VMEM)] * len(operands),
+        out_specs=[pl.BlockSpec(memory_space=pltpu.VMEM)] * len(outs),
+    )(slots, *operands)
+
+
+def unit_rows(block):
+    wide = block.astype(F32)
+    scale = lax.rsqrt(jnp.mean(wide * wide, axis=-1, keepdims=True) + EPS)
+    return wide * scale, scale
+
+
+def norm_kernel(block, gain, out):
+    out[...] = (unit_rows(block[...])[0] * gain[...]).astype(BF16)
+
+
+def normalize(block, gain):
+    return call(norm_kernel, [(block.shape, BF16)], [], [], [block, gain], [], 1)[0]
+
+
+def norm_back_kernel(kept, near, far, block, gain, upstream, out):
+    unit, scale = unit_rows(block[...])
+    grad_normed = kept[...] + near[...].astype(F32) + far[...].astype(F32)
+    weighted = grad_normed * gain[...]
     inner = jnp.mean(weighted * unit, axis=-1, keepdims=True)
-    return (upstream.astype(F32) + scale * (weighted - unit * inner)).astype(BF16)
+    out[...] = (upstream[0].astype(F32) + scale * (weighted - unit * inner)).astype(BF16)
+
+
+def norm_back(kept, near, far, block, gain, upstream):
+    return call(
+        norm_back_kernel, [(block.shape, BF16)], [], [], [kept, near, far, block, gain, upstream], [], 1
+    )[0]
 
 
 def back_project(grads, weight):
@@ -292,41 +337,28 @@
     sections = lax.axis_size("section")
     is_early = section_idx < sections // 2
     rows = x_fwd.shape[1]
-    gain = norm_gain[0]
     weight_q = w_query[0]
     weight_k = w_keyval[0, 0]
     weight_v = w_keyval[0, 1]
-    held = stash[0]
-
-    def start_gather(block, tag):
-        with jax.named_scope(tag + "_far"):
-            far = chip_swap(block, 2)
-        with jax.named_scope(tag + "_near"):
-            near = chip_swap(block, 1)
-        return block, near, far
-
-    def pass_on(far, tag):
-        with jax.named_scope(tag + "_last"):
-            return chip_swap(far, 1)
+
+    def send(value, mask, tag):
+        with jax.named_scope(tag):
+            return chip_swap(value, mask)
 
     def swap(value, tag):
-        with jax.named_scope(tag + "_swap"):
+        with jax.named_scope(tag):
             return core_swap(value)
 
-    own2, near2, far2 = start_gather(grad_in[0], "g2")
+    with jax.named_scope("payload"):
+        payload = with_slots(payload_kernel, [x_fwd.shape[1:]], slot_table, x_fwd, stash)[0]
+        received = lax.ppermute(payload, "section", [(i, sections - 1 - i) for i in range(sections)])
     with jax.named_scope("norm_fwd"):
-        normed_fwd, _, _ = normalize(x_fwd[0], gain)
-    own1, near1, far1 = start_gather(normed_fwd, "g1")
-    with jax.named_scope("payload"):
-        returned = lax.dynamic_index_in_dim(held, slot_table[0, 0], 0, keepdims=False)
-        payload = jnp.where(is_early, x_fwd[0], returned)
-        received = lax.ppermute(
-            after(payload, normed_fwd), "section", [(i, sections - 1 - i) for i in range(sections)]
-        )
-    last1 = pass_on(far1, "g1")
-    last2 = pass_on(after(far2, far1), "g2")
-    mine1 = [own1, near1, far1, last1]
-    mine2 = [own2, near2, far2, last2]
+        own1 = normalize(after(x_fwd[0], payload), norm_gain)
+    far1 = send(own1, 2, "g1_far")
+    near1 = send(own1, 1, "g1_near")
+    last1 = send(far1, 1, "g1_last")
+    own2 = grad_in[0]
+    far2 = send(own2, 2, "g2_far")
 
     with jax.named_scope("tables"):
         position = local_positions(rows)
@@ -335,49 +367,43 @@
         cosine, sine = jnp.concatenate([cosine, cosine], axis=1), jnp.concatenate([-sine, sine], axis=1)
 
     with jax.named_scope("norm_bwd"):
-        received = after(received, near1, near2, last1, last2)
-        own_block = lax.dynamic_index_in_dim(held, slot_table[0, 1], 0, keepdims=False)
-        checkpoint = jnp.where(is_early, received, own_block)
-        normed_bwd, unit, scale = normalize(checkpoint, gain)
-    own3, near3, far3 = start_gather(normed_bwd, "g3")
+        received, far2 = lax.optimization_barrier((received, far2, near1, last1))[:2]
+        checkpoint, own3 = with_slots(
+            checkpoint_kernel, [received.shape] * 2, slot_table, received, stash, norm_gain
+        )
+    far3 = send(own3, 2, "g3_far")
+    near3 = send(own3, 1, "g3_near")
+    pair2 = jnp.concatenate([own2, far2], axis=0)
+    near2 = send(pair2, 1, "g2_near")
 
     with jax.named_scope("qkv_fwd"):
-        pieces = mine1 + [swap(piece, "g1") for piece in mine1]
-        pieces = [after(pieces[0], normed_bwd)] + pieces[1:]
+        mine = jnp.concatenate([own1, far1, near1], axis=0)
+        pieces = [mine, last1, swap(mine, "g1_swap"), swap(last1, "g1_swaplast")]
+        pieces = [after(pieces[0], own3)] + pieces[1:]
         query, keys, values = qkv(pieces, w_query, w_keyval, cosine, sine)
     with jax.named_scope("attn_fwd"):
         part_own, part_other = attn_fwd(query, keys, values, mask, w_out)
-    with jax.named_scope("r1_swap"):
-        part_other = after(part_other, near3, far3)
-        swapped1 = core_swap(part_other)
-    last3 = pass_on(after(far3, part_other), "g3")
-    mine3 = [own3, near3, far3, last3]
+    swapped1 = swap(part_other, "r1_swap")
+    far3, near3, near2 = lax.optimization_barrier((far3, near3, near2, part_other))[:3]
+    last3 = send(far3, 1, "g3_last")
+    kept1, far1_sum, near1_sum, pass1 = scatter_parts(part_own, swapped1)
+    pass1 = pass1.astype(BF16)
+    from_near1 = send(pass1, 1, "r1_pass")
     with jax.named_scope("grad_mixed"):
-        pieces = mine2 + [swap(piece, "g2") for piece in mine2]
-        pieces = [after(pieces[0], part_other)] + pieces[1:]
+        pieces = [after(pair2, pass1), near2, swap(pair2, "g2_swap"), swap(near2, "g2_swapnear")]
         grad_mixed = grad_mixing(pieces, w_out)
-    kept1, near1_sum, far1_sum, pass1 = scatter_parts(part_own, swapped1)
-    with jax.named_scope("r1_pass"):
-        from_near1 = chip_swap(pass1.astype(BF16), 1)
-    from_near1 = after(from_near1, last3)
-    with jax.named_scope("r1_far"):
-        sum_far1 = chip_swap((far1_sum + from_near1.astype(F32)).astype(BF16), 2)
-    with jax.named_scope("r1_near"):
-        sum_near1 = chip_swap(after(near1_sum, from_near1).astype(BF16), 1)
+    from_near1, last3, grad_mixed = lax.optimization_barrier((from_near1, last3, grad_mixed))
+    sum_far1 = send((far1_sum + from_near1.astype(F32)).astype(BF16), 2, "r1_far")
+    sum_near1 = send(after(near1_sum, from_near1).astype(BF16), 1, "r1_near")
 
     with jax.named_scope("qkv_bwd"):
-        pieces = mine3 + [swap(piece, "g3") for piece in mine3]
+        mine = jnp.concatenate([own3, far3, near3], axis=0)
+        pieces = [mine, last3, swap(mine, "g3_swap"), swap(last3, "g3_swaplast")]
         pieces = [after(pieces[0], from_near1)] + pieces[1:]
         query_b, keys_b, values_b = qkv(pieces, w_query, w_keyval, cosine, sine)
     with jax.named_scope("attn_bwd"):
         grads = attn_bwd(query_b, keys_b, values_b, grad_mixed, mask, cosine, sine)
 
-    with jax.named_scope("fwd_out"):
-        attn_part = kept1 + after(sum_near1, grads[0]).astype(F32) + after(sum_far1, grads[0]).astype(F32)
-        output = (x_fwd[0].astype(F32) + attn_part).astype(BF16)
-        fwd_out = shifted(output[None], 1)
-    grads = lax.optimization_barrier((output, *grads))[1:]
-
     half = 4 * rows
 
     def grad_rows(low, high):
@@ -389,23 +415,23 @@
         back_other = grad_rows(half, 2 * half).astype(BF16)
     with jax.named_scope("back_own"):
         back_own = grad_rows(0, half)
-    with jax.named_scope("r2_swap"):
-        swapped2 = core_swap(back_other)
-    kept2, near2_sum, far2_sum, pass2 = scatter_parts(back_own, swapped2)
-    with jax.named_scope("r2_pass"):
-        from_near2 = chip_swap(pass2.astype(BF16), 1)
-    with jax.named_scope("r2_far"):
-        sum_far2 = chip_swap((far2_sum + from_near2.astype(F32)).astype(BF16), 2)
-    with jax.named_scope("r2_near"):
-        sum_near2 = chip_swap(after(near2_sum, from_near2).astype(BF16), 1)
-
+    swapped2 = swap(back_other, "r2_swap")
+    kept2, far2_sum, near2_sum, pass2 = scatter_parts(back_own, swapped2)
+    pass2 = pass2.astype(BF16)
+    from_near2 = send(pass2, 1, "r2_pass")
+    sum_far2 = send((far2_sum + from_near2.astype(F32)).astype(BF16), 2, "r2_far")
+    sum_near2 = send(after(near2_sum, from_near2).astype(BF16), 1, "r2_near")
+
+    with jax.named_scope("fwd_out"):
+        attn_part = kept1 + after(sum_near1, pass2).astype(F32) + after(sum_far1, pass2).astype(F32)
+        output = (x_fwd[0].astype(F32) + attn_part).astype(BF16)
+        fwd_out = shifted(output[None], 1)
     with jax.named_scope("stash_out"):
-        slot_ids = jnp.arange(held.shape[0], dtype=jnp.int32)
+        slot_ids = jnp.arange(stash.shape[1], dtype=jnp.int32)
         replace = jnp.logical_and(slot_ids == slot_table[0, 0], jnp.logical_not(is_early))
-        stash_out = jnp.where(replace[:, None, None], received[None], held)[None]
+        stash_out = jnp.where(replace[:, None, None], received[None], stash[0])[None]
     with jax.named_scope("bwd_out"):
-        grad_normed = kept2 + sum_near2.astype(F32) + sum_far2.astype(F32)
-        grad_x = norm_back(grad_normed, unit, scale, gain, grad_in[0])
+        grad_x = norm_back(kept2, sum_near2, sum_far2, checkpoint, norm_gain, grad_in)
         bwd_out = shifted(grad_x[None], -1)
     return (fwd_out, bwd_out, stash_out)
 

time: 160 us -> 149 us (0.931)
  other arithmetic: 12.2 us -> 6.16 us
  Pallas kernels: 16.3 us -> 21.9 us
  waiting for transfers between devices: 74.2 us -> 69.8 us
  between operations: 4.62 us -> 1 us
    ppermute x15 -> x14, waiting for transfers between devices: 47.5 us -> 43.4 us  [chip_swap(): lax.ppermute(value, 'tensor', [(i, i ^ 2 * mask) for i in range(size)])]
    pallas_call x0 -> x2, Pallas kernels: none -> 3.91 us  [with_slots(): pl.pallas_call(kernel, out_shape=[jax.ShapeDtypeStruct(shape, BF16) for s...]
    reduce_sum x3 -> x0, other arithmetic: 3.77 us -> none  [the longest x2 2.34 us: normalize(): scale = lax.rsqrt(jnp.mean(wide * wide, axis=-1, keepdims=True) + EPS)]
    concatenate x0 -> x2, other arithmetic: none -> 2.86 us  [the longest x1 1.78 us: body(): pair2 = jnp.concatenate([own2, far2], axis=0)]
    ppermute x14 -> x8, waiting for transfers between devices: 3.27 us -> 0.78 us  [core_swap(): return lax.ppermute(value, 'tensor', [(i, i ^ 1) for i in range(size)])]
    ppermute x1, waiting for transfers between devices: 10.9 us -> 13 us  [body(): lax.ppermute(payload, 'section', [(i, sections - 1 - i) for i in range(se...]
    select_n x2 -> x1, other arithmetic: 3.62 us -> 1.86 us  [body(): jnp.where(replace[:, None, None], received[None], stash[0])[None]]
    pallas_call x5 -> x7, Pallas kernels: 16.3 us -> 18 us  [call(): pl.pallas_call(kernel, out_shape=[jax.ShapeDtypeStruct(shape, dtype) for...]
  transfers between devices with their start and end apart: 32 -> 25, of which waited for: 15 -> 14; matrix products, arithmetic and copies ran while one was open for 9% -> 8% of each run, Pallas kernels for 10% -> 14%
where the time goes in v2:
time: 149 us; the launch traced here: 147 us
  waiting for transfers between devices  69.8 us (47%)
  starting transfers between devices  37.6 us (25%)
  Pallas kernels  21.9 us (15%)
  other arithmetic  6.16 us (4%)
  local copies, waits for them, and re-layouts  5.54 us (4%)
  matrix products  4.73 us (3%)
    ppermute x14, waiting for transfers between devices, chip_swap(): lax.ppermute(value, 'tensor', [(i, i ^ 2 * mask) for i in range(size)])  43.4 us
    ppermute x14, starting transfers between devices, chip_swap(): lax.ppermute(value, 'tensor', [(i, i ^ 2 * mask) for i in range(size)])  22.5 us
    pallas_call x7, Pallas kernels, call(): pl.pallas_call(kernel, out_shape=[jax.ShapeDtypeStruct(shape, dtype) for...  18 us
    ppermute x1, waiting for transfers between devices, body(): lax.ppermute(payload, 'section', [(i, sections - 1 - i) for i in range(se...  13 us
    ppermute x2, waiting for transfers between devices, shifted(): lax.ppermute(value, 'section', [(i, i + steps) for i in range(count) if 0...  12.6 us
    ppermute x2, starting transfers between devices, shifted(): lax.ppermute(value, 'section', [(i, i + steps) for i in range(count) if 0...  8.35 us
    unnamed x32, local copies, waits for them, and re-layouts  5.35 us
    ppermute x1, starting transfers between devices, body(): lax.ppermute(payload, 'section', [(i, sections - 1 - i) for i in range(se...  4.97 us
  transfers between devices with their start and end apart: 25, of which 14 were waited for; matrix products, arithmetic and copies ran while one was open for 8% of the time, Pallas kernels for 14%

profile of v2, /device:TPU:62, one launch (start us, length us, event | category | flops | bytes accessed | tf_op | source)
XLA Modules:
  0.0 146.8 jit_solution(15897351167966830055)
XLA Ops:
  0.6 1.9 %payload.1 = bf16[32,4096]{1,0:T(8,128)(2,1)} custom-call(s32[1,2]{1,0:T(1,128)} %slots.3, bf16[1,32,4096]{2,1,0:T(8,128)(2,1)} %x.1, bf16[1,2,32,4096]{3,2,1,0:T(8,128)(2,1)} %held.3), custom_call_target="tpu_custom_call" | custom-call | tf_op jit(solution)/shard_map/payload/pallas_call | solution.py:295
  4.4 3.4 %collective-permute-start = (bf16[32,4096]{1,0:T(8,128)(2,1)S(1)}, bf16[32,4096]{1,0:T(8,128)(2,1)}, u32[]{:S(2)}, u32[]{:S(2)}) collective-permute-start(bf16[32,4096]{1,0:T(8,128)(2,1)S(1)} %norm_fwd.1), channel_id=1, source_target_pairs={{0,4},{1,5},{2,6},{3,7},{4,0},{5,1},{6,2},{7,3},{8,12},{9,13},{10,... | collective-permute-start | bytes 786440 | tf_op jit(solution)/shard_map/g1_far/ppermute | solution.py:25
  7.8 5.0 %collective-permute-start.2 = (bf16[32,4096]{1,0:T(8,128)(2,1)}, bf16[32,4096]{1,0:T(8,128)(2,1)}, u32[]{:S(2)}, u32[]{:S(2)}) collective-permute-start(bf16[32,4096]{1,0:T(8,128)(2,1)} %payload.1), channel_id=1, source_target_pairs={{0,248},{8,240},{16,232},{24,224},{32,216},{40,208},{48,200},{56,1... | collective-permute-start | bytes 786440 | tf_op jit(solution)/shard_map/payload/ppermute | solution.py:354
  15.2 5.2 %collective-permute-done = bf16[32,4096]{1,0:T(8,128)(2,1)} collective-permute-done((bf16[32,4096]{1,0:T(8,128)(2,1)S(1)}, bf16[32,4096]{1,0:T(8,128)(2,1)}, u32[]{:S(2)}, u32[]{:S(2)}) %collective-permute-start) | collective-permute-done | bytes 262176 | tf_op jit(solution)/shard_map/g1_far/ppermute | solution.py:25
  23.0 13.0 %collective-permute-done.2.received = bf16[32,4096]{1,0:T(8,128)(2,1)} collective-permute-done((bf16[32,4096]{1,0:T(8,128)(2,1)}, bf16[32,4096]{1,0:T(8,128)(2,1)}, u32[]{:S(2)}, u32[]{:S(2)}) %collective-permute-start.2) | collective-permute-done | bytes 262176 | tf_op jit(solution)/shard_map/payload/ppermute | solution.py:354
  36.0 5.1 %collective-permute-done.3 = bf16[32,4096]{1,0:T(8,128)(2,1)} collective-permute-done((bf16[32,4096]{1,0:T(8,128)(2,1)}, bf16[32,4096]{1,0:T(8,128)(2,1)}, u32[]{:S(2)}, u32[]{:S(2)}) %collective-permute-start.3) | collective-permute-done | bytes 262176 | tf_op jit(solution)/shard_map/g2_far/ppermute | solution.py:25
  44.3 2.0 %norm_bwd.1 = (bf16[32,4096]{1,0:T(8,128)(2,1)}, bf16[32,4096]{1,0:T(8,128)(2,1)}) custom-call(s32[1,2]{1,0:T(1,128)} %slots.3, bf16[32,4096]{1,0:T(8,128)(2,1)} %collective-permute-done.2.received, bf16[1,2,32,4096]{3,2,1,0:T(8,128)(2,1)} %held.3, f32[1,4096]{1,0:T(1,128)} %gain.5), custom_call_target="tpu_custom_call" | custom-call | tf_op jit(solution)/shard_map/norm_bwd/pallas_call | solution.py:295
  48.0 5.2 %collective-permute-start.9 = (bf16[32,4096]{1,0:T(8,128)(2,1)}, bf16[32,4096]{1,0:T(8,128)(2,1)S(1)}, u32[]{:S(2)}, u32[]{:S(2)}) collective-permute-start(bf16[32,4096]{1,0:T(8,128)(2,1)} %get-tuple-element.34), channel_id=1, source_target_pairs={{0,4},{1,5},{2,6},{3,7},{4,0},{5,1},{6,2},{7,3},{8,12},{9,13},{10,... | collective-permute-start | bytes 786440 | tf_op jit(solution)/shard_map/g3_far/ppermute | solution.py:25
  53.2 2.2 %copy-done = bf16[1,4096,512]{2,1,0:T(8,128)(2,1)S(1)} copy-done((bf16[1,4096,512]{2,1,0:T(8,128)(2,1)S(1)}, bf16[1,4096,512]{2,1,0:T(8,128)(2,1)}, u32[]{:S(2)}) %copy-start) | copy-done | bytes 4194328
  55.4 4.5 %qkv_fwd.1 = (bf16[256,512]{1,0:T(8,128)(2,1)S(1)}, bf16[256,128]{1,0:T(8,128)(2,1)S(1)}, bf16[256,128]{1,0:T(8,128)(2,1)S(1)}) custom-call(bf16[96,4096]{1,0:T(8,128)(2,1)S(1)} %pad_maximum_fusion.refs_0_, bf16[32,4096]{1,0:T(8,128)(2,1)} %collective-permute-done.4.refs_1_, bf16[96,4096]{1,0:T(8,128)(2,1)} %collective-permute-done.5.refs_2_, ...), custom_call_target="tpu_custom_call" | custom-call | flops 25165824 | bytes 65536 | tf_op jit(solution)/shard_map/qkv_fwd/pallas_call | solution.py:190
  59.9 2.8 %attn_fwd.1 = (f32[128,4096]{1,0:T(8,128)S(1)}, bf16[128,4096]{1,0:T(8,128)(2,1)S(1)}) custom-call(bf16[1,512,4096]{2,1,0:T(8,128)(2,1)S(1)} %copy-done.3, bf16[256,512]{1,0:T(8,128)(2,1)S(1)} %get-tuple-element.36.q, bf16[256,128]{1,0:T(8,128)(2,1)S(1)} %get-tuple-element.37.k, bf16[256,128]{1,0:T(8,128)(2,1)S(1)} %get-tuple-element.38.v, ...), custom_call_target="tpu_custom_call" | custom-call | flops 16777216 | bytes 65536 | tf_op jit(solution)/shard_map/attn_fwd/pallas_call | solution.py:190
  63.6 4.2 %collective-permute-done.10 = bf16[32,4096]{1,0:T(8,128)(2,1)S(1)} collective-permute-done((bf16[32,4096]{1,0:T(8,128)(2,1)}, bf16[32,4096]{1,0:T(8,128)(2,1)S(1)}, u32[]{:S(2)}, u32[]{:S(2)}) %collective-permute-start.10) | collective-permute-done | bytes 262176 | tf_op jit(solution)/shard_map/g3_near/ppermute | solution.py:25
  67.7 5.4 %collective-permute-done.9 = bf16[32,4096]{1,0:T(8,128)(2,1)S(1)} collective-permute-done((bf16[32,4096]{1,0:T(8,128)(2,1)}, bf16[32,4096]{1,0:T(8,128)(2,1)S(1)}, u32[]{:S(2)}, u32[]{:S(2)}) %collective-permute-start.9) | collective-permute-done | bytes 262176 | tf_op jit(solution)/shard_map/g3_far/ppermute | solution.py:25
  73.8 2.1 %collective-permute-start.8 = (bf16[32,4096]{1,0:T(8,128)(2,1)S(1)}, bf16[32,4096]{1,0:T(8,128)(2,1)S(1)}, u32[]{:S(2)}, u32[]{:S(2)}) collective-permute-start(bf16[32,4096]{1,0:T(8,128)(2,1)S(1)} %add_convert_fusion.2), channel_id=1, source_target_pairs={{0,2},{1,3},{2,0},{3,1},{4,6},{5,7},{6,4},{7,5},{8,10},{9,11},{10,... | collective-permute-start | bytes 786440 | tf_op jit(solution)/shard_map/r1_pass/ppermute | solution.py:25
  76.5 4.0 %grad_mixed.1.gm = bf16[256,512]{1,0:T(8,128)(2,1)S(1)} custom-call(bf16[64,4096]{1,0:T(8,128)(2,1)} %pad_maximum_fusion.1.refs_0_, bf16[64,4096]{1,0:T(8,128)(2,1)} %collective-permute-done.11.refs_1_, bf16[64,4096]{1,0:T(8,128)(2,1)S(1)} %collective-permute-done.13.refs_2_, bf16[64,4096]{1,0:T(8,128)(2,1)S(1)} %collective-permute-done.14.refs_3_, ...), custom_call_target="tpu_custom_call" | custom-call | flops 16777216 | bytes 65536 | tf_op jit(solution)/shard_map/grad_mixed/pallas_call | solution.py:190
  82.3 4.6 %collective-permute-done.8 = bf16[32,4096]{1,0:T(8,128)(2,1)S(1)} collective-permute-done((bf16[32,4096]{1,0:T(8,128)(2,1)S(1)}, bf16[32,4096]{1,0:T(8,128)(2,1)S(1)}, u32[]{:S(2)}, u32[]{:S(2)}) %collective-permute-start.8) | collective-permute-done | bytes 262176 | tf_op jit(solution)/shard_map/r1_pass/ppermute | solution.py:25
  88.9 3.8 %qkv_bwd.1 = (bf16[256,512]{1,0:T(8,128)(2,1)S(1)}, bf16[256,128]{1,0:T(8,128)(2,1)S(1)}, bf16[256,128]{1,0:T(8,128)(2,1)S(1)}) custom-call(bf16[96,4096]{1,0:T(8,128)(2,1)S(1)} %constant_dynamic-update-slice_fusion.refs_0_, bf16[32,4096]{1,0:T(8,128)(2,1)S(1)} %collective-permute-done.12.refs_1_, bf16[96,4096]{1,0:T(8,128)(2,1)S(1)} %collective-permute-done.16.refs_2_, ...), custom_call_target="tpu_custom_call" | custom-call | flops 25165824 | bytes 65536 | tf_op jit(solution)/shard_map/qkv_bwd/pallas_call | solution.py:190
  92.7 2.3 %attn_bwd.1 = (bf16[256,512]{1,0:T(8,128)(2,1)S(1)}, bf16[256,128]{1,0:T(8,128)(2,1)S(1)}, bf16[256,128]{1,0:T(8,128)(2,1)S(1)}) custom-call(bf16[256,512]{1,0:T(8,128)(2,1)S(1)} %get-tuple-element.50.q, bf16[256,128]{1,0:T(8,128)(2,1)S(1)} %get-tuple-element.51.k, bf16[256,128]{1,0:T(8,128)(2,1)S(1)} %get-tuple-element.52.v, ...), custom_call_target="tpu_custom_call" | custom-call | flops 8388608 | bytes 65536 | tf_op jit(solution)/shard_map/attn_bwd/pallas_call | solution.py:190
  102.4 6.6 %collective-permute-done.21 = bf16[32,4096]{1,0:T(8,128)(2,1)S(1)} collective-permute-done((bf16[32,4096]{1,0:T(8,128)(2,1)S(1)}, bf16[32,4096]{1,0:T(8,128)(2,1)S(1)}, u32[]{:S(2)}, u32[]{:S(2)}) %collective-permute-start.21) | collective-permute-done | bytes 262176 | tf_op jit(solution)/shard_map/r2_pass/ppermute | solution.py:25
  112.5 6.4 %collective-permute-start.20 = (bf16[1,32,4096]{2,1,0:T(8,128)(2,1)S(1)}, bf16[1,32,4096]{2,1,0:T(8,128)(2,1)S(1)}, u32[]{:S(2)}, u32[]{:S(2)}) collective-permute-start(bf16[1,32,4096]{2,1,0:T(8,128)(2,1)S(1)} %fusion.16), channel_id=1, source_target_pairs={{0,8},{8,16},{16,24},{24,32},{32,40},{40,48},{48,56},{56,64},{64,7... | collective-permute-start | bytes 786440 | tf_op jit(solution)/shard_map/fwd_out/ppermute | solution.py:30
  118.9 4.8 %collective-permute-done.22.near = bf16[32,4096]{1,0:T(8,128)(2,1)S(1)} collective-permute-done((bf16[32,4096]{1,0:T(8,128)(2,1)S(1)}, bf16[32,4096]{1,0:T(8,128)(2,1)S(1)}, u32[]{:S(2)}, u32[]{:S(2)}) %collective-permute-start.22) | collective-permute-done | bytes 262176 | tf_op jit(solution)/shard_map/r2_near/ppermute | solution.py:25
  123.8 4.8 %collective-permute-done.23.far = bf16[32,4096]{1,0:T(8,128)(2,1)S(1)} collective-permute-done((bf16[32,4096]{1,0:T(8,128)(2,1)S(1)}, bf16[32,4096]{1,0:T(8,128)(2,1)S(1)}, u32[]{:S(2)}, u32[]{:S(2)}) %collective-permute-start.23) | collective-permute-done | bytes 262176 | tf_op jit(solution)/shard_map/r2_far/ppermute | solution.py:25
  129.0 1.9 %collective-permute-start.24 = (bf16[1,32,4096]{2,1,0:T(8,128)(2,1)S(1)}, bf16[1,32,4096]{2,1,0:T(8,128)(2,1)S(1)}, u32[]{:S(2)}, u32[]{:S(2)}) collective-permute-start(bf16[1,32,4096]{2,1,0:T(8,128)(2,1)S(1)} %bitcast.34), channel_id=1, source_target_pairs={{8,0},{16,8},{24,16},{32,24},{40,32},{48,40},{56,48},{64,56},{72,6... | collective-permute-start | bytes 786440 | tf_op jit(solution)/shard_map/bwd_out/ppermute | solution.py:30
  132.8 12.6 %collective-permute-done.24 = bf16[1,32,4096]{2,1,0:T(8,128)(2,1)S(1)} collective-permute-done((bf16[1,32,4096]{2,1,0:T(8,128)(2,1)S(1)}, bf16[1,32,4096]{2,1,0:T(8,128)(2,1)S(1)}, u32[]{:S(2)}, u32[]{:S(2)}) %collective-permute-start.24) | collective-permute-done | bytes 262176 | tf_op jit(solution)/shard_map/bwd_out/ppermute | solution.py:30
  (94 shorter events, 32.1 us)
Async XLA Ops:
  4.4 16.1 %collective-permute-start = (bf16[32,4096]{1,0:T(8,128)(2,1)S(1)}, bf16[32,4096]{1,0:T(8,128)(2,1)}, u32[]{:S(2)}, u32[]{:S(2)}) collective-permute-start(bf16[32,4096]{1,0:T(8,128)(2,1)S(1)} %norm_fwd.1), channel_id=1, source_target_pairs={{0,4},{1,5},{2,6},{3,7},{4,0},{5,1},{6,2},{7,3},{8,12},{9,13},{10,... | collective-permute-start | bytes 786440 | tf_op jit(solution)/shard_map/g1_far/ppermute | solution.py:25
  7.7 14.0 %collective-permute-start.1 = (bf16[32,4096]{1,0:T(8,128)(2,1)S(1)}, bf16[32,4096]{1,0:T(8,128)(2,1)}, u32[]{:S(2)}, u32[]{:S(2)}) collective-permute-start(bf16[32,4096]{1,0:T(8,128)(2,1)S(1)} %norm_fwd.1), channel_id=1, source_target_pairs={{0,2},{1,3},{2,0},{3,1},{4,6},{5,7},{6,4},{7,5},{8,10},{9,11},{10,... | collective-permute-start | bytes 786440 | tf_op jit(solution)/shard_map/g1_near/ppermute | solution.py:25
  7.8 28.2 %collective-permute-start.2 = (bf16[32,4096]{1,0:T(8,128)(2,1)}, bf16[32,4096]{1,0:T(8,128)(2,1)}, u32[]{:S(2)}, u32[]{:S(2)}) collective-permute-start(bf16[32,4096]{1,0:T(8,128)(2,1)} %payload.1), channel_id=1, source_target_pairs={{0,248},{8,240},{16,232},{24,224},{32,216},{40,208},{48,200},{56,1... | collective-permute-start | bytes 786440 | tf_op jit(solution)/shard_map/payload/ppermute | solution.py:354
  12.8 28.3 %collective-permute-start.3 = (bf16[32,4096]{1,0:T(8,128)(2,1)}, bf16[32,4096]{1,0:T(8,128)(2,1)}, u32[]{:S(2)}, u32[]{:S(2)}) collective-permute-start(bf16[32,4096]{1,0:T(8,128)(2,1)} %bitcast.32), channel_id=1, source_target_pairs={{0,4},{1,5},{2,6},{3,7},{4,0},{5,1},{6,2},{7,3},{8,12},{9,13},{10,... | collective-permute-start | bytes 786440 | tf_op jit(solution)/shard_map/g2_far/ppermute | solution.py:25
  20.4 21.7 %collective-permute-start.4 = (bf16[32,4096]{1,0:T(8,128)(2,1)}, bf16[32,4096]{1,0:T(8,128)(2,1)}, u32[]{:S(2)}, u32[]{:S(2)}) collective-permute-start(bf16[32,4096]{1,0:T(8,128)(2,1)} %collective-permute-done), channel_id=1, source_target_pairs={{0,2},{1,3},{2,0},{3,1},{4,6},{5,7},{6,4},{7,5},{8,10},{9,11},{10,... | collective-permute-start | bytes 786440 | tf_op jit(solution)/shard_map/g1_last/ppermute | solution.py:25
  22.8 30.4 %collective-permute-start.5 = (bf16[96,4096]{1,0:T(8,128)(2,1)S(1)}, bf16[96,4096]{1,0:T(8,128)(2,1)}, u32[]{:S(2)}, u32[]{:S(2)}) collective-permute-start(bf16[96,4096]{1,0:T(8,128)(2,1)S(1)} %pad_maximum_fusion.refs_0_), channel_id=1, source_target_pairs={{0,1},{1,0},{2,3},{3,2},{4,5},{5,4},{6,7},{7,6},{8,9},{9,8},{10,11... | collective-permute-start | bytes 2359304 | tf_op jit(solution)/shard_map/qkv_fwd/g1_swap/ppermute | solution.py:20
  42.1 11.1 %collective-permute-start.6 = (bf16[32,4096]{1,0:T(8,128)(2,1)}, bf16[32,4096]{1,0:T(8,128)(2,1)}, u32[]{:S(2)}, u32[]{:S(2)}) collective-permute-start(bf16[32,4096]{1,0:T(8,128)(2,1)} %collective-permute-done.4.refs_1_), channel_id=1, source_target_pairs={{0,1},{1,0},{2,3},{3,2},{4,5},{5,4},{6,7},{7,6},{8,9},{9,8},{10,11... | collective-permute-start | bytes 786440 | tf_op jit(solution)/shard_map/qkv_fwd/g1_swaplast/ppermute | solution.py:20
  43.9 29.2 %collective-permute-start.11 = (bf16[64,4096]{1,0:T(8,128)(2,1)}, bf16[64,4096]{1,0:T(8,128)(2,1)}, u32[]{:S(2)}, u32[]{:S(2)}) collective-permute-start(bf16[64,4096]{1,0:T(8,128)(2,1)} %pad_maximum_fusion.1.refs_0_), channel_id=1, source_target_pairs={{0,2},{1,3},{2,0},{3,1},{4,6},{5,7},{6,4},{7,5},{8,10},{9,11},{10,... | collective-permute-start | bytes 1572872 | tf_op jit(solution)/shard_map/g2_near/ppermute | solution.py:25
  46.4 21.3 %collective-permute-start.10 = (bf16[32,4096]{1,0:T(8,128)(2,1)}, bf16[32,4096]{1,0:T(8,128)(2,1)S(1)}, u32[]{:S(2)}, u32[]{:S(2)}) collective-permute-start(bf16[32,4096]{1,0:T(8,128)(2,1)} %get-tuple-element.34), channel_id=1, source_target_pairs={{0,2},{1,3},{2,0},{3,1},{4,6},{5,7},{6,4},{7,5},{8,10},{9,11},{10,... | collective-permute-start | bytes 786440 | tf_op jit(solution)/shard_map/g3_near/ppermute | solution.py:25
  48.0 25.1 %collective-permute-start.9 = (bf16[32,4096]{1,0:T(8,128)(2,1)}, bf16[32,4096]{1,0:T(8,128)(2,1)S(1)}, u32[]{:S(2)}, u32[]{:S(2)}) collective-permute-start(bf16[32,4096]{1,0:T(8,128)(2,1)} %get-tuple-element.34), channel_id=1, source_target_pairs={{0,4},{1,5},{2,6},{3,7},{4,0},{5,1},{6,2},{7,3},{8,12},{9,13},{10,... | collective-permute-start | bytes 786440 | tf_op jit(solution)/shard_map/g3_far/ppermute | solution.py:25
  62.7 11.1 %collective-permute-start.7 = (bf16[128,4096]{1,0:T(8,128)(2,1)S(1)}, bf16[128,4096]{1,0:T(8,128)(2,1)S(1)}, u32[]{:S(2)}, u32[]{:S(2)}) collective-permute-start(bf16[128,4096]{1,0:T(8,128)(2,1)S(1)} %get-tuple-element.40), channel_id=1, source_target_pairs={{0,1},{1,0},{2,3},{3,2},{4,5},{5,4},{6,7},{7,6},{8,9},{9,8},{10,11... | collective-permute-start | bytes 3145736 | tf_op jit(solution)/shard_map/r1_swap/ppermute | solution.py:20
  62.8 13.2 %collective-permute-start.13 = (bf16[64,4096]{1,0:T(8,128)(2,1)}, bf16[64,4096]{1,0:T(8,128)(2,1)S(1)}, u32[]{:S(2)}, u32[]{:S(2)}) collective-permute-start(bf16[64,4096]{1,0:T(8,128)(2,1)} %pad_maximum_fusion.1.refs_0_), channel_id=1, source_target_pairs={{0,1},{1,0},{2,3},{3,2},{4,5},{5,4},{6,7},{7,6},{8,9},{9,8},{10,11... | collective-permute-start | bytes 1572872 | tf_op jit(solution)/shard_map/grad_mixed/g2_swap/ppermute | solution.py:20
  73.1 9.2 %collective-permute-start.12 = (bf16[32,4096]{1,0:T(8,128)(2,1)S(1)}, bf16[32,4096]{1,0:T(8,128)(2,1)S(1)}, u32[]{:S(2)}, u32[]{:S(2)}) collective-permute-start(bf16[32,4096]{1,0:T(8,128)(2,1)S(1)} %collective-permute-done.9), channel_id=1, source_target_pairs={{0,2},{1,3},{2,0},{3,1},{4,6},{5,7},{6,4},{7,5},{8,10},{9,11},{10,... | collective-permute-start | bytes 786440 | tf_op jit(solution)/shard_map/g3_last/ppermute | solution.py:25
  73.1 15.7 %collective-permute-start.16 = (bf16[96,4096]{1,0:T(8,128)(2,1)S(1)}, bf16[96,4096]{1,0:T(8,128)(2,1)S(1)}, u32[]{:S(2)}, u32[]{:S(2)}) collective-permute-start(bf16[96,4096]{1,0:T(8,128)(2,1)S(1)} %constant_dynamic-update-slice_fusion.refs_0_), channel_id=1, source_target_pairs={{0,1},{1,0},{2,3},{3,2},{4,5},{5,4},{6,7},{7,6},{8,9},{9,8},{10,11... | collective-permute-start | bytes 2359304 | tf_op jit(solution)/shard_map/qkv_bwd/g3_swap/ppermute | solution.py:20
  73.2 3.2 %collective-permute-start.14 = (bf16[64,4096]{1,0:T(8,128)(2,1)}, bf16[64,4096]{1,0:T(8,128)(2,1)S(1)}, u32[]{:S(2)}, u32[]{:S(2)}) collective-permute-start(bf16[64,4096]{1,0:T(8,128)(2,1)} %collective-permute-done.11.refs_1_), channel_id=1, source_target_pairs={{0,1},{1,0},{2,3},{3,2},{4,5},{5,4},{6,7},{7,6},{8,9},{9,8},{10,11... | collective-permute-start | bytes 1572872 | tf_op jit(solution)/shard_map/grad_mixed/g2_swapnear/ppermute | solution.py:20
  73.8 13.1 %collective-permute-start.8 = (bf16[32,4096]{1,0:T(8,128)(2,1)S(1)}, bf16[32,4096]{1,0:T(8,128)(2,1)S(1)}, u32[]{:S(2)}, u32[]{:S(2)}) collective-permute-start(bf16[32,4096]{1,0:T(8,128)(2,1)S(1)} %add_convert_fusion.2), channel_id=1, source_target_pairs={{0,2},{1,3},{2,0},{3,1},{4,6},{5,7},{6,4},{7,5},{8,10},{9,11},{10,... | collective-permute-start | bytes 786440 | tf_op jit(solution)/shard_map/r1_pass/ppermute | solution.py:25
  86.9 15.5 %collective-permute-start.15 = (bf16[32,4096]{1,0:T(8,128)(2,1)S(1)}, bf16[32,4096]{1,0:T(8,128)(2,1)S(1)}, u32[]{:S(2)}, u32[]{:S(2)}) collective-permute-start(bf16[32,4096]{1,0:T(8,128)(2,1)S(1)} %convert_add_fusion), channel_id=1, source_target_pairs={{0,2},{1,3},{2,0},{3,1},{4,6},{5,7},{6,4},{7,5},{8,10},{9,11},{10,... | collective-permute-start | bytes 786440 | tf_op jit(solution)/shard_map/r1_near/ppermute | solution.py:25
  87.2 15.1 %collective-permute-start.19 = (bf16[32,4096]{1,0:T(8,128)(2,1)S(1)}, bf16[32,4096]{1,0:T(8,128)(2,1)S(1)}, u32[]{:S(2)}, u32[]{:S(2)}) collective-permute-start(bf16[32,4096]{1,0:T(8,128)(2,1)S(1)} %add_convert_fusion.1), channel_id=1, source_target_pairs={{0,4},{1,5},{2,6},{3,7},{4,0},{5,1},{6,2},{7,3},{8,12},{9,13},{10,... | collective-permute-start | bytes 786440 | tf_op jit(solution)/shard_map/r1_far/ppermute | solution.py:25
  97.4 3.0 %collective-permute-start.18 = (bf16[128,4096]{1,0:T(8,128)(2,1)S(1)}, bf16[128,4096]{1,0:T(8,128)(2,1)S(1)}, u32[]{:S(2)}, u32[]{:S(2)}) collective-permute-start(bf16[128,4096]{1,0:T(8,128)(2,1)S(1)} %fusion), channel_id=1, source_target_pairs={{0,1},{1,0},{2,3},{3,2},{4,5},{5,4},{6,7},{7,6},{8,9},{9,8},{10,11... | collective-permute-start | bytes 3145736 | tf_op jit(solution)/shard_map/r2_swap/ppermute | solution.py:20
  100.4 8.5 %collective-permute-start.21 = (bf16[32,4096]{1,0:T(8,128)(2,1)S(1)}, bf16[32,4096]{1,0:T(8,128)(2,1)S(1)}, u32[]{:S(2)}, u32[]{:S(2)}) collective-permute-start(bf16[32,4096]{1,0:T(8,128)(2,1)S(1)} %fusion.15), channel_id=1, source_target_pairs={{0,2},{1,3},{2,0},{3,1},{4,6},{5,7},{6,4},{7,5},{8,10},{9,11},{10,... | collective-permute-start | bytes 786440 | tf_op jit(solution)/shard_map/r2_pass/ppermute | solution.py:25
  109.0 14.8 %collective-permute-start.22 = (bf16[32,4096]{1,0:T(8,128)(2,1)S(1)}, bf16[32,4096]{1,0:T(8,128)(2,1)S(1)}, u32[]{:S(2)}, u32[]{:S(2)}) collective-permute-start(bf16[32,4096]{1,0:T(8,128)(2,1)S(1)} %slice_add_fusion.1), channel_id=1, source_target_pairs={{0,2},{1,3},{2,0},{3,1},{4,6},{5,7},{6,4},{7,5},{8,10},{9,11},{10,... | collective-permute-start | bytes 786440 | tf_op jit(solution)/shard_map/r2_near/ppermute | solution.py:25
  110.9 17.7 %collective-permute-start.23 = (bf16[32,4096]{1,0:T(8,128)(2,1)S(1)}, bf16[32,4096]{1,0:T(8,128)(2,1)S(1)}, u32[]{:S(2)}, u32[]{:S(2)}) collective-permute-start(bf16[32,4096]{1,0:T(8,128)(2,1)S(1)} %get-tuple-element.61), channel_id=1, source_target_pairs={{0,4},{1,5},{2,6},{3,7},{4,0},{5,1},{6,2},{7,3},{8,12},{9,13},{10,... | collective-permute-start | bytes 786440 | tf_op jit(solution)/shard_map/r2_far/ppermute | solution.py:25
  112.5 20.3 %collective-permute-start.20 = (bf16[1,32,4096]{2,1,0:T(8,128)(2,1)S(1)}, bf16[1,32,4096]{2,1,0:T(8,128)(2,1)S(1)}, u32[]{:S(2)}, u32[]{:S(2)}) collective-permute-start(bf16[1,32,4096]{2,1,0:T(8,128)(2,1)S(1)} %fusion.16), channel_id=1, source_target_pairs={{0,8},{8,16},{16,24},{24,32},{32,40},{40,48},{48,56},{56,64},{64,7... | collective-permute-start | bytes 786440 | tf_op jit(solution)/shard_map/fwd_out/ppermute | solution.py:30
  129.0 16.4 %collective-permute-start.24 = (bf16[1,32,4096]{2,1,0:T(8,128)(2,1)S(1)}, bf16[1,32,4096]{2,1,0:T(8,128)(2,1)S(1)}, u32[]{:S(2)}, u32[]{:S(2)}) collective-permute-start(bf16[1,32,4096]{2,1,0:T(8,128)(2,1)S(1)} %bitcast.34), channel_id=1, source_target_pairs={{8,0},{16,8},{24,16},{32,24},{40,32},{48,40},{56,48},{64,56},{72,6... | collective-permute-start | bytes 786440 | tf_op jit(solution)/shard_map/bwd_out/ppermute | solution.py:30
  (15 other events, 241.8 us)

commit v3 on v2

--- a/solution.py
+++ b/solution.py
@@ -425,7 +425,12 @@
     with jax.named_scope("fwd_out"):
         attn_part = kept1 + after(sum_near1, pass2).astype(F32) + after(sum_far1, pass2).astype(F32)
         output = (x_fwd[0].astype(F32) + attn_part).astype(BF16)
-        fwd_out = shifted(output[None], 1)
+        middle = sections // 2
+        hops = [(i, 0 if i == middle - 1 else i + 1) for i in range(sections - 1)]
+        first = lax.ppermute(output[None], "section", hops)
+        second = lax.ppermute(first, "section", [(0, middle)])
+        kept_first = jnp.where(section_idx == 0, jnp.zeros_like(first), first)
+        fwd_out = jnp.where(section_idx == middle, second, kept_first)
     with jax.named_scope("stash_out"):
         slot_ids = jnp.arange(stash.shape[1], dtype=jnp.int32)
         replace = jnp.logical_and(slot_ids == slot_table[0, 0], jnp.logical_not(is_early))

time: 149 us -> 147 us (0.987); the launches traced: 147 us -> 147 us
  starting transfers between devices: 37.6 us -> 34.8 us
  waiting for transfers between devices: 69.8 us -> 72.6 us
    ppermute x2 -> x1, waiting for transfers between devices: 12.6 us -> 18.7 us  [shifted(): lax.ppermute(value, 'section', [(i, i + steps) for i in range(count) if 0...]
    ppermute x2 -> x1, starting transfers between devices: 8.35 us -> 2.74 us  [shifted(): lax.ppermute(value, 'section', [(i, i + steps) for i in range(count) if 0...]
    ppermute x14, waiting for transfers between devices: 43.4 us -> 39.8 us  [chip_swap(): lax.ppermute(value, 'tensor', [(i, i ^ 2 * mask) for i in range(size)])]
    ppermute x0 -> x2, starting transfers between devices: none -> 2.8 us  [the longest x1 2.13 us: body(): first = lax.ppermute(output[None], 'section', hops)]
    unnamed x32 -> x31, local copies, waits for them, and re-layouts: 5.35 us -> 4.65 us
  transfers between devices with their start and end apart: 25 -> 26, of which waited for: 14 -> 15; matrix products, arithmetic and copies ran while one was open for 8% -> 8% of each run, Pallas kernels for 14% -> 14%
where the time goes in v3:
time: 147 us
  waiting for transfers between devices  72.6 us (49%)
  starting transfers between devices  34.8 us (24%)
  Pallas kernels  21.9 us (15%)
  other arithmetic  6.92 us (5%)
  local copies, waits for them, and re-layouts  4.83 us (3%)
  matrix products  4.73 us (3%)
    ppermute x14, waiting for transfers between devices, chip_swap(): lax.ppermute(value, 'tensor', [(i, i ^ 2 * mask) for i in range(size)])  39.8 us
    ppermute x14, starting transfers between devices, chip_swap(): lax.ppermute(value, 'tensor', [(i, i ^ 2 * mask) for i in range(size)])  22.5 us
    ppermute x1, waiting for transfers between devices, shifted(): lax.ppermute(value, 'section', [(i, i + steps) for i in range(count) if 0...  18.7 us
    pallas_call x7, Pallas kernels, call(): pl.pallas_call(kernel, out_shape=[jax.ShapeDtypeStruct(shape, dtype) for...  18 us
    ppermute x1, waiting for transfers between devices, body(): lax.ppermute(payload, 'section', [(i, sections - 1 - i) for i in range(se...  13 us
    ppermute x1, starting transfers between devices, body(): lax.ppermute(payload, 'section', [(i, sections - 1 - i) for i in range(se...  4.97 us
    dot_general x6, matrix products, back_project(): return jnp.einsum('tq,dq->td', grads, weight, preferred_element_type=F32)  4.73 us
    unnamed x31, local copies, waits for them, and re-layouts  4.65 us
  transfers between devices with their start and end apart: 26, of which 15 were waited for; matrix products, arithmetic and copies ran while one was open for 8% of the time, Pallas kernels for 14%

profile of v3, /device:TPU:62, one launch (start us, length us, event | category | flops | bytes accessed | tf_op | source)
XLA Modules:
  0.0 146.8 jit_solution(10073596118999620646)
XLA Ops:
  0.6 1.9 %payload.1 = bf16[32,4096]{1,0:T(8,128)(2,1)} custom-call(s32[1,2]{1,0:T(1,128)} %slots.3, bf16[1,32,4096]{2,1,0:T(8,128)(2,1)} %x.1, bf16[1,2,32,4096]{3,2,1,0:T(8,128)(2,1)} %held.3), custom_call_target="tpu_custom_call" | custom-call | tf_op jit(solution)/shard_map/payload/pallas_call | solution.py:295
  4.4 3.4 %collective-permute-start = (bf16[32,4096]{1,0:T(8,128)(2,1)S(1)}, bf16[32,4096]{1,0:T(8,128)(2,1)}, u32[]{:S(2)}, u32[]{:S(2)}) collective-permute-start(bf16[32,4096]{1,0:T(8,128)(2,1)S(1)} %norm_fwd.1), channel_id=1, source_target_pairs={{0,4},{1,5},{2,6},{3,7},{4,0},{5,1},{6,2},{7,3},{8,12},{9,13},{10,... | collective-permute-start | bytes 786440 | tf_op jit(solution)/shard_map/g1_far/ppermute | solution.py:25
  7.8 5.0 %collective-permute-start.2 = (bf16[32,4096]{1,0:T(8,128)(2,1)}, bf16[32,4096]{1,0:T(8,128)(2,1)}, u32[]{:S(2)}, u32[]{:S(2)}) collective-permute-start(bf16[32,4096]{1,0:T(8,128)(2,1)} %payload.1), channel_id=1, source_target_pairs={{0,248},{8,240},{16,232},{24,224},{32,216},{40,208},{48,200},{56,1... | collective-permute-start | bytes 786440 | tf_op jit(solution)/shard_map/payload/ppermute | solution.py:354
  15.2 5.2 %collective-permute-done = bf16[32,4096]{1,0:T(8,128)(2,1)} collective-permute-done((bf16[32,4096]{1,0:T(8,128)(2,1)S(1)}, bf16[32,4096]{1,0:T(8,128)(2,1)}, u32[]{:S(2)}, u32[]{:S(2)}) %collective-permute-start) | collective-permute-done | bytes 262176 | tf_op jit(solution)/shard_map/g1_far/ppermute | solution.py:25
  23.0 13.0 %collective-permute-done.2.received = bf16[32,4096]{1,0:T(8,128)(2,1)} collective-permute-done((bf16[32,4096]{1,0:T(8,128)(2,1)}, bf16[32,4096]{1,0:T(8,128)(2,1)}, u32[]{:S(2)}, u32[]{:S(2)}) %collective-permute-start.2) | collective-permute-done | bytes 262176 | tf_op jit(solution)/shard_map/payload/ppermute | solution.py:354
  36.0 5.1 %collective-permute-done.3 = bf16[32,4096]{1,0:T(8,128)(2,1)} collective-permute-done((bf16[32,4096]{1,0:T(8,128)(2,1)}, bf16[32,4096]{1,0:T(8,128)(2,1)}, u32[]{:S(2)}, u32[]{:S(2)}) %collective-permute-start.3) | collective-permute-done | bytes 262176 | tf_op jit(solution)/shard_map/g2_far/ppermute | solution.py:25
  44.3 2.0 %norm_bwd.1 = (bf16[32,4096]{1,0:T(8,128)(2,1)}, bf16[32,4096]{1,0:T(8,128)(2,1)}) custom-call(s32[1,2]{1,0:T(1,128)} %slots.3, bf16[32,4096]{1,0:T(8,128)(2,1)} %collective-permute-done.2.received, bf16[1,2,32,4096]{3,2,1,0:T(8,128)(2,1)} %held.3, f32[1,4096]{1,0:T(1,128)} %gain.5), custom_call_target="tpu_custom_call" | custom-call | tf_op jit(solution)/shard_map/norm_bwd/pallas_call | solution.py:295
  48.0 5.2 %collective-permute-start.9 = (bf16[32,4096]{1,0:T(8,128)(2,1)}, bf16[32,4096]{1,0:T(8,128)(2,1)S(1)}, u32[]{:S(2)}, u32[]{:S(2)}) collective-permute-start(bf16[32,4096]{1,0:T(8,128)(2,1)} %get-tuple-element.34), channel_id=1, source_target_pairs={{0,4},{1,5},{2,6},{3,7},{4,0},{5,1},{6,2},{7,3},{8,12},{9,13},{10,... | collective-permute-start | bytes 786440 | tf_op jit(solution)/shard_map/g3_far/ppermute | solution.py:25
  53.2 2.2 %copy-done = bf16[1,4096,512]{2,1,0:T(8,128)(2,1)S(1)} copy-done((bf16[1,4096,512]{2,1,0:T(8,128)(2,1)S(1)}, bf16[1,4096,512]{2,1,0:T(8,128)(2,1)}, u32[]{:S(2)}) %copy-start) | copy-done | bytes 4194328
  55.4 4.5 %qkv_fwd.1 = (bf16[256,512]{1,0:T(8,128)(2,1)S(1)}, bf16[256,128]{1,0:T(8,128)(2,1)S(1)}, bf16[256,128]{1,0:T(8,128)(2,1)S(1)}) custom-call(bf16[96,4096]{1,0:T(8,128)(2,1)S(1)} %pad_maximum_fusion.refs_0_, bf16[32,4096]{1,0:T(8,128)(2,1)} %collective-permute-done.4.refs_1_, bf16[96,4096]{1,0:T(8,128)(2,1)} %collective-permute-done.5.refs_2_, ...), custom_call_target="tpu_custom_call" | custom-call | flops 25165824 | bytes 65536 | tf_op jit(solution)/shard_map/qkv_fwd/pallas_call | solution.py:190
  59.9 2.8 %attn_fwd.1 = (f32[128,4096]{1,0:T(8,128)S(1)}, bf16[128,4096]{1,0:T(8,128)(2,1)S(1)}) custom-call(bf16[1,512,4096]{2,1,0:T(8,128)(2,1)S(1)} %copy-done.3, bf16[256,512]{1,0:T(8,128)(2,1)S(1)} %get-tuple-element.36.q, bf16[256,128]{1,0:T(8,128)(2,1)S(1)} %get-tuple-element.37.k, bf16[256,128]{1,0:T(8,128)(2,1)S(1)} %get-tuple-element.38.v, ...), custom_call_target="tpu_custom_call" | custom-call | flops 16777216 | bytes 65536 | tf_op jit(solution)/shard_map/attn_fwd/pallas_call | solution.py:190
  63.6 4.2 %collective-permute-done.10 = bf16[32,4096]{1,0:T(8,128)(2,1)S(1)} collective-permute-done((bf16[32,4096]{1,0:T(8,128)(2,1)}, bf16[32,4096]{1,0:T(8,128)(2,1)S(1)}, u32[]{:S(2)}, u32[]{:S(2)}) %collective-permute-start.10) | collective-permute-done | bytes 262176 | tf_op jit(solution)/shard_map/g3_near/ppermute | solution.py:25
  67.7 5.4 %collective-permute-done.9 = bf16[32,4096]{1,0:T(8,128)(2,1)S(1)} collective-permute-done((bf16[32,4096]{1,0:T(8,128)(2,1)}, bf16[32,4096]{1,0:T(8,128)(2,1)S(1)}, u32[]{:S(2)}, u32[]{:S(2)}) %collective-permute-start.9) | collective-permute-done | bytes 262176 | tf_op jit(solution)/shard_map/g3_far/ppermute | solution.py:25
  73.8 2.1 %collective-permute-start.8 = (bf16[32,4096]{1,0:T(8,128)(2,1)S(1)}, bf16[32,4096]{1,0:T(8,128)(2,1)S(1)}, u32[]{:S(2)}, u32[]{:S(2)}) collective-permute-start(bf16[32,4096]{1,0:T(8,128)(2,1)S(1)} %add_convert_fusion.2), channel_id=1, source_target_pairs={{0,2},{1,3},{2,0},{3,1},{4,6},{5,7},{6,4},{7,5},{8,10},{9,11},{10,... | collective-permute-start | bytes 786440 | tf_op jit(solution)/shard_map/r1_pass/ppermute | solution.py:25
  76.5 4.0 %grad_mixed.1.gm = bf16[256,512]{1,0:T(8,128)(2,1)S(1)} custom-call(bf16[64,4096]{1,0:T(8,128)(2,1)} %pad_maximum_fusion.1.refs_0_, bf16[64,4096]{1,0:T(8,128)(2,1)} %collective-permute-done.11.refs_1_, bf16[64,4096]{1,0:T(8,128)(2,1)S(1)} %collective-permute-done.13.refs_2_, bf16[64,4096]{1,0:T(8,128)(2,1)S(1)} %collective-permute-done.14.refs_3_, ...), custom_call_target="tpu_custom_call" | custom-call | flops 16777216 | bytes 65536 | tf_op jit(solution)/shard_map/grad_mixed/pallas_call | solution.py:190
  82.3 4.6 %collective-permute-done.8 = bf16[32,4096]{1,0:T(8,128)(2,1)S(1)} collective-permute-done((bf16[32,4096]{1,0:T(8,128)(2,1)S(1)}, bf16[32,4096]{1,0:T(8,128)(2,1)S(1)}, u32[]{:S(2)}, u32[]{:S(2)}) %collective-permute-start.8) | collective-permute-done | bytes 262176 | tf_op jit(solution)/shard_map/r1_pass/ppermute | solution.py:25
  88.9 3.8 %qkv_bwd.1 = (bf16[256,512]{1,0:T(8,128)(2,1)S(1)}, bf16[256,128]{1,0:T(8,128)(2,1)S(1)}, bf16[256,128]{1,0:T(8,128)(2,1)S(1)}) custom-call(bf16[96,4096]{1,0:T(8,128)(2,1)S(1)} %constant_dynamic-update-slice_fusion.refs_0_, bf16[32,4096]{1,0:T(8,128)(2,1)S(1)} %collective-permute-done.12.refs_1_, bf16[96,4096]{1,0:T(8,128)(2,1)S(1)} %collective-permute-done.16.refs_2_, ...), custom_call_target="tpu_custom_call" | custom-call | flops 25165824 | bytes 65536 | tf_op jit(solution)/shard_map/qkv_bwd/pallas_call | solution.py:190
  92.7 2.3 %attn_bwd.1 = (bf16[256,512]{1,0:T(8,128)(2,1)S(1)}, bf16[256,128]{1,0:T(8,128)(2,1)S(1)}, bf16[256,128]{1,0:T(8,128)(2,1)S(1)}) custom-call(bf16[256,512]{1,0:T(8,128)(2,1)S(1)} %get-tuple-element.50.q, bf16[256,128]{1,0:T(8,128)(2,1)S(1)} %get-tuple-element.51.k, bf16[256,128]{1,0:T(8,128)(2,1)S(1)} %get-tuple-element.52.v, ...), custom_call_target="tpu_custom_call" | custom-call | flops 8388608 | bytes 65536 | tf_op jit(solution)/shard_map/attn_bwd/pallas_call | solution.py:190
  102.4 2.1 %collective-permute-start.20 = (bf16[1,32,4096]{2,1,0:T(8,128)(2,1)S(1)}, bf16[1,32,4096]{2,1,0:T(8,128)(2,1)S(1)}, u32[]{:S(2)}, u32[]{:S(2)}) collective-permute-start(bf16[1,32,4096]{2,1,0:T(8,128)(2,1)S(1)} %fusion.16), channel_id=1, source_target_pairs={{0,8},{8,16},{16,24},{24,32},{32,40},{40,48},{48,56},{56,64},{64,7... | collective-permute-start | bytes 786440 | tf_op jit(solution)/shard_map/fwd_out/ppermute | solution.py:430
  104.7 4.3 %collective-permute-done.22 = bf16[32,4096]{1,0:T(8,128)(2,1)S(1)} collective-permute-done((bf16[32,4096]{1,0:T(8,128)(2,1)S(1)}, bf16[32,4096]{1,0:T(8,128)(2,1)S(1)}, u32[]{:S(2)}, u32[]{:S(2)}) %collective-permute-start.22) | collective-permute-done | bytes 262176 | tf_op jit(solution)/shard_map/r2_pass/ppermute | solution.py:25
  115.2 6.1 %collective-permute-done.23.near = bf16[32,4096]{1,0:T(8,128)(2,1)S(1)} collective-permute-done((bf16[32,4096]{1,0:T(8,128)(2,1)S(1)}, bf16[32,4096]{1,0:T(8,128)(2,1)S(1)}, u32[]{:S(2)}, u32[]{:S(2)}) %collective-permute-start.23) | collective-permute-done | bytes 262176 | tf_op jit(solution)/shard_map/r2_near/ppermute | solution.py:25
  121.3 2.2 %collective-permute-done.24.far = bf16[32,4096]{1,0:T(8,128)(2,1)S(1)} collective-permute-done((bf16[32,4096]{1,0:T(8,128)(2,1)S(1)}, bf16[32,4096]{1,0:T(8,128)(2,1)S(1)}, u32[]{:S(2)}, u32[]{:S(2)}) %collective-permute-start.24) | collective-permute-done | bytes 262176 | tf_op jit(solution)/shard_map/r2_far/ppermute | solution.py:25
  123.9 2.7 %collective-permute-start.25 = (bf16[1,32,4096]{2,1,0:T(8,128)(2,1)S(1)}, bf16[1,32,4096]{2,1,0:T(8,128)(2,1)S(1)}, u32[]{:S(2)}, u32[]{:S(2)}) collective-permute-start(bf16[1,32,4096]{2,1,0:T(8,128)(2,1)S(1)} %bitcast.34), channel_id=1, source_target_pairs={{8,0},{16,8},{24,16},{32,24},{40,32},{48,40},{56,48},{64,56},{72,6... | collective-permute-start | bytes 786440 | tf_op jit(solution)/shard_map/bwd_out/ppermute | solution.py:30
  127.4 18.7 %collective-permute-done.25 = bf16[1,32,4096]{2,1,0:T(8,128)(2,1)S(1)} collective-permute-done((bf16[1,32,4096]{2,1,0:T(8,128)(2,1)S(1)}, bf16[1,32,4096]{2,1,0:T(8,128)(2,1)S(1)}, u32[]{:S(2)}, u32[]{:S(2)}) %collective-permute-start.25) | collective-permute-done | bytes 262176 | tf_op jit(solution)/shard_map/bwd_out/ppermute | solution.py:30
  (96 shorter events, 33.2 us)
Async XLA Ops:
  4.4 16.1 %collective-permute-start = (bf16[32,4096]{1,0:T(8,128)(2,1)S(1)}, bf16[32,4096]{1,0:T(8,128)(2,1)}, u32[]{:S(2)}, u32[]{:S(2)}) collective-permute-start(bf16[32,4096]{1,0:T(8,128)(2,1)S(1)} %norm_fwd.1), channel_id=1, source_target_pairs={{0,4},{1,5},{2,6},{3,7},{4,0},{5,1},{6,2},{7,3},{8,12},{9,13},{10,... | collective-permute-start | bytes 786440 | tf_op jit(solution)/shard_map/g1_far/ppermute | solution.py:25
  7.7 14.0 %collective-permute-start.1 = (bf16[32,4096]{1,0:T(8,128)(2,1)S(1)}, bf16[32,4096]{1,0:T(8,128)(2,1)}, u32[]{:S(2)}, u32[]{:S(2)}) collective-permute-start(bf16[32,4096]{1,0:T(8,128)(2,1)S(1)} %norm_fwd.1), channel_id=1, source_target_pairs={{0,2},{1,3},{2,0},{3,1},{4,6},{5,7},{6,4},{7,5},{8,10},{9,11},{10,... | collective-permute-start | bytes 786440 | tf_op jit(solution)/shard_map/g1_near/ppermute | solution.py:25
  7.8 28.2 %collective-permute-start.2 = (bf16[32,4096]{1,0:T(8,128)(2,1)}, bf16[32,4096]{1,0:T(8,128)(2,1)}, u32[]{:S(2)}, u32[]{:S(2)}) collective-permute-start(bf16[32,4096]{1,0:T(8,128)(2,1)} %payload.1), channel_id=1, source_target_pairs={{0,248},{8,240},{16,232},{24,224},{32,216},{40,208},{48,200},{56,1... | collective-permute-start | bytes 786440 | tf_op jit(solution)/shard_map/payload/ppermute | solution.py:354
  12.8 28.3 %collective-permute-start.3 = (bf16[32,4096]{1,0:T(8,128)(2,1)}, bf16[32,4096]{1,0:T(8,128)(2,1)}, u32[]{:S(2)}, u32[]{:S(2)}) collective-permute-start(bf16[32,4096]{1,0:T(8,128)(2,1)} %bitcast.32), channel_id=1, source_target_pairs={{0,4},{1,5},{2,6},{3,7},{4,0},{5,1},{6,2},{7,3},{8,12},{9,13},{10,... | collective-permute-start | bytes 786440 | tf_op jit(solution)/shard_map/g2_far/ppermute | solution.py:25
  20.4 21.7 %collective-permute-start.4 = (bf16[32,4096]{1,0:T(8,128)(2,1)}, bf16[32,4096]{1,0:T(8,128)(2,1)}, u32[]{:S(2)}, u32[]{:S(2)}) collective-permute-start(bf16[32,4096]{1,0:T(8,128)(2,1)} %collective-permute-done), channel_id=1, source_target_pairs={{0,2},{1,3},{2,0},{3,1},{4,6},{5,7},{6,4},{7,5},{8,10},{9,11},{10,... | collective-permute-start | bytes 786440 | tf_op jit(solution)/shard_map/g1_last/ppermute | solution.py:25
  22.8 30.4 %collective-permute-start.5 = (bf16[96,4096]{1,0:T(8,128)(2,1)S(1)}, bf16[96,4096]{1,0:T(8,128)(2,1)}, u32[]{:S(2)}, u32[]{:S(2)}) collective-permute-start(bf16[96,4096]{1,0:T(8,128)(2,1)S(1)} %pad_maximum_fusion.refs_0_), channel_id=1, source_target_pairs={{0,1},{1,0},{2,3},{3,2},{4,5},{5,4},{6,7},{7,6},{8,9},{9,8},{10,11... | collective-permute-start | bytes 2359304 | tf_op jit(solution)/shard_map/qkv_fwd/g1_swap/ppermute | solution.py:20
  42.1 11.1 %collective-permute-start.6 = (bf16[32,4096]{1,0:T(8,128)(2,1)}, bf16[32,4096]{1,0:T(8,128)(2,1)}, u32[]{:S(2)}, u32[]{:S(2)}) collective-permute-start(bf16[32,4096]{1,0:T(8,128)(2,1)} %collective-permute-done.4.refs_1_), channel_id=1, source_target_pairs={{0,1},{1,0},{2,3},{3,2},{4,5},{5,4},{6,7},{7,6},{8,9},{9,8},{10,11... | collective-permute-start | bytes 786440 | tf_op jit(solution)/shard_map/qkv_fwd/g1_swaplast/ppermute | solution.py:20
  43.9 29.2 %collective-permute-start.11 = (bf16[64,4096]{1,0:T(8,128)(2,1)}, bf16[64,4096]{1,0:T(8,128)(2,1)}, u32[]{:S(2)}, u32[]{:S(2)}) collective-permute-start(bf16[64,4096]{1,0:T(8,128)(2,1)} %pad_maximum_fusion.1.refs_0_), channel_id=1, source_target_pairs={{0,2},{1,3},{2,0},{3,1},{4,6},{5,7},{6,4},{7,5},{8,10},{9,11},{10,... | collective-permute-start | bytes 1572872 | tf_op jit(solution)/shard_map/g2_near/ppermute | solution.py:25
  46.4 21.3 %collective-permute-start.10 = (bf16[32,4096]{1,0:T(8,128)(2,1)}, bf16[32,4096]{1,0:T(8,128)(2,1)S(1)}, u32[]{:S(2)}, u32[]{:S(2)}) collective-permute-start(bf16[32,4096]{1,0:T(8,128)(2,1)} %get-tuple-element.34), channel_id=1, source_target_pairs={{0,2},{1,3},{2,0},{3,1},{4,6},{5,7},{6,4},{7,5},{8,10},{9,11},{10,... | collective-permute-start | bytes 786440 | tf_op jit(solution)/shard_map/g3_near/ppermute | solution.py:25
  48.0 25.1 %collective-permute-start.9 = (bf16[32,4096]{1,0:T(8,128)(2,1)}, bf16[32,4096]{1,0:T(8,128)(2,1)S(1)}, u32[]{:S(2)}, u32[]{:S(2)}) collective-permute-start(bf16[32,4096]{1,0:T(8,128)(2,1)} %get-tuple-element.34), channel_id=1, source_target_pairs={{0,4},{1,5},{2,6},{3,7},{4,0},{5,1},{6,2},{7,3},{8,12},{9,13},{10,... | collective-permute-start | bytes 786440 | tf_op jit(solution)/shard_map/g3_far/ppermute | solution.py:25
  62.7 11.1 %collective-permute-start.7 = (bf16[128,4096]{1,0:T(8,128)(2,1)S(1)}, bf16[128,4096]{1,0:T(8,128)(2,1)S(1)}, u32[]{:S(2)}, u32[]{:S(2)}) collective-permute-start(bf16[128,4096]{1,0:T(8,128)(2,1)S(1)} %get-tuple-element.40), channel_id=1, source_target_pairs={{0,1},{1,0},{2,3},{3,2},{4,5},{5,4},{6,7},{7,6},{8,9},{9,8},{10,11... | collective-permute-start | bytes 3145736 | tf_op jit(solution)/shard_map/r1_swap/ppermute | solution.py:20
  62.8 13.2 %collective-permute-start.13 = (bf16[64,4096]{1,0:T(8,128)(2,1)}, bf16[64,4096]{1,0:T(8,128)(2,1)S(1)}, u32[]{:S(2)}, u32[]{:S(2)}) collective-permute-start(bf16[64,4096]{1,0:T(8,128)(2,1)} %pad_maximum_fusion.1.refs_0_), channel_id=1, source_target_pairs={{0,1},{1,0},{2,3},{3,2},{4,5},{5,4},{6,7},{7,6},{8,9},{9,8},{10,11... | collective-permute-start | bytes 1572872 | tf_op jit(solution)/shard_map/grad_mixed/g2_swap/ppermute | solution.py:20
  73.1 9.2 %collective-permute-start.12 = (bf16[32,4096]{1,0:T(8,128)(2,1)S(1)}, bf16[32,4096]{1,0:T(8,128)(2,1)S(1)}, u32[]{:S(2)}, u32[]{:S(2)}) collective-permute-start(bf16[32,4096]{1,0:T(8,128)(2,1)S(1)} %collective-permute-done.9), channel_id=1, source_target_pairs={{0,2},{1,3},{2,0},{3,1},{4,6},{5,7},{6,4},{7,5},{8,10},{9,11},{10,... | collective-permute-start | bytes 786440 | tf_op jit(solution)/shard_map/g3_last/ppermute | solution.py:25
  73.1 15.7 %collective-permute-start.16 = (bf16[96,4096]{1,0:T(8,128)(2,1)S(1)}, bf16[96,4096]{1,0:T(8,128)(2,1)S(1)}, u32[]{:S(2)}, u32[]{:S(2)}) collective-permute-start(bf16[96,4096]{1,0:T(8,128)(2,1)S(1)} %constant_dynamic-update-slice_fusion.refs_0_), channel_id=1, source_target_pairs={{0,1},{1,0},{2,3},{3,2},{4,5},{5,4},{6,7},{7,6},{8,9},{9,8},{10,11... | collective-permute-start | bytes 2359304 | tf_op jit(solution)/shard_map/qkv_bwd/g3_swap/ppermute | solution.py:20
  73.2 3.2 %collective-permute-start.14 = (bf16[64,4096]{1,0:T(8,128)(2,1)}, bf16[64,4096]{1,0:T(8,128)(2,1)S(1)}, u32[]{:S(2)}, u32[]{:S(2)}) collective-permute-start(bf16[64,4096]{1,0:T(8,128)(2,1)} %collective-permute-done.11.refs_1_), channel_id=1, source_target_pairs={{0,1},{1,0},{2,3},{3,2},{4,5},{5,4},{6,7},{7,6},{8,9},{9,8},{10,11... | collective-permute-start | bytes 1572872 | tf_op jit(solution)/shard_map/grad_mixed/g2_swapnear/ppermute | solution.py:20
  73.8 13.1 %collective-permute-start.8 = (bf16[32,4096]{1,0:T(8,128)(2,1)S(1)}, bf16[32,4096]{1,0:T(8,128)(2,1)S(1)}, u32[]{:S(2)}, u32[]{:S(2)}) collective-permute-start(bf16[32,4096]{1,0:T(8,128)(2,1)S(1)} %add_convert_fusion.2), channel_id=1, source_target_pairs={{0,2},{1,3},{2,0},{3,1},{4,6},{5,7},{6,4},{7,5},{8,10},{9,11},{10,... | collective-permute-start | bytes 786440 | tf_op jit(solution)/shard_map/r1_pass/ppermute | solution.py:25
  86.9 15.4 %collective-permute-start.15 = (bf16[32,4096]{1,0:T(8,128)(2,1)S(1)}, bf16[32,4096]{1,0:T(8,128)(2,1)S(1)}, u32[]{:S(2)}, u32[]{:S(2)}) collective-permute-start(bf16[32,4096]{1,0:T(8,128)(2,1)S(1)} %convert_add_fusion), channel_id=1, source_target_pairs={{0,2},{1,3},{2,0},{3,1},{4,6},{5,7},{6,4},{7,5},{8,10},{9,11},{10,... | collective-permute-start | bytes 786440 | tf_op jit(solution)/shard_map/r1_near/ppermute | solution.py:25
  87.2 15.0 %collective-permute-start.19 = (bf16[32,4096]{1,0:T(8,128)(2,1)S(1)}, bf16[32,4096]{1,0:T(8,128)(2,1)S(1)}, u32[]{:S(2)}, u32[]{:S(2)}) collective-permute-start(bf16[32,4096]{1,0:T(8,128)(2,1)S(1)} %add_convert_fusion.1), channel_id=1, source_target_pairs={{0,4},{1,5},{2,6},{3,7},{4,0},{5,1},{6,2},{7,3},{8,12},{9,13},{10,... | collective-permute-start | bytes 786440 | tf_op jit(solution)/shard_map/r1_far/ppermute | solution.py:25
  100.4 8.6 %collective-permute-start.22 = (bf16[32,4096]{1,0:T(8,128)(2,1)S(1)}, bf16[32,4096]{1,0:T(8,128)(2,1)S(1)}, u32[]{:S(2)}, u32[]{:S(2)}) collective-permute-start(bf16[32,4096]{1,0:T(8,128)(2,1)S(1)} %fusion.15), channel_id=1, source_target_pairs={{0,2},{1,3},{2,0},{3,1},{4,6},{5,7},{6,4},{7,5},{8,10},{9,11},{10,... | collective-permute-start | bytes 786440 | tf_op jit(solution)/shard_map/r2_pass/ppermute | solution.py:25
  102.4 10.2 %collective-permute-start.20 = (bf16[1,32,4096]{2,1,0:T(8,128)(2,1)S(1)}, bf16[1,32,4096]{2,1,0:T(8,128)(2,1)S(1)}, u32[]{:S(2)}, u32[]{:S(2)}) collective-permute-start(bf16[1,32,4096]{2,1,0:T(8,128)(2,1)S(1)} %fusion.16), channel_id=1, source_target_pairs={{0,8},{8,16},{16,24},{24,32},{32,40},{40,48},{48,56},{56,64},{64,7... | collective-permute-start | bytes 786440 | tf_op jit(solution)/shard_map/fwd_out/ppermute | solution.py:430
  109.0 12.3 %collective-permute-start.23 = (bf16[32,4096]{1,0:T(8,128)(2,1)S(1)}, bf16[32,4096]{1,0:T(8,128)(2,1)S(1)}, u32[]{:S(2)}, u32[]{:S(2)}) collective-permute-start(bf16[32,4096]{1,0:T(8,128)(2,1)S(1)} %slice_add_fusion.1), channel_id=1, source_target_pairs={{0,2},{1,3},{2,0},{3,1},{4,6},{5,7},{6,4},{7,5},{8,10},{9,11},{10,... | collective-permute-start | bytes 786440 | tf_op jit(solution)/shard_map/r2_near/ppermute | solution.py:25
  110.8 12.6 %collective-permute-start.24 = (bf16[32,4096]{1,0:T(8,128)(2,1)S(1)}, bf16[32,4096]{1,0:T(8,128)(2,1)S(1)}, u32[]{:S(2)}, u32[]{:S(2)}) collective-permute-start(bf16[32,4096]{1,0:T(8,128)(2,1)S(1)} %get-tuple-element.61), channel_id=1, source_target_pairs={{0,4},{1,5},{2,6},{3,7},{4,0},{5,1},{6,2},{7,3},{8,12},{9,13},{10,... | collective-permute-start | bytes 786440 | tf_op jit(solution)/shard_map/r2_far/ppermute | solution.py:25
  112.7 14.0 %collective-permute-start.21 = (bf16[1,32,4096]{2,1,0:T(8,128)(2,1)S(1)}, bf16[1,32,4096]{2,1,0:T(8,128)(2,1)S(1)}, u32[]{:S(2)}, u32[]{:S(2)}) collective-permute-start(bf16[1,32,4096]{2,1,0:T(8,128)(2,1)S(1)} %collective-permute-done.20), channel_id=1, source_target_pairs={{0,128},{1,129},{2,130},{3,131},{4,132},{5,133},{6,134},{7,135}} | collective-permute-start | bytes 786440 | tf_op jit(solution)/shard_map/fwd_out/ppermute | solution.py:431
  123.9 22.2 %collective-permute-start.25 = (bf16[1,32,4096]{2,1,0:T(8,128)(2,1)S(1)}, bf16[1,32,4096]{2,1,0:T(8,128)(2,1)S(1)}, u32[]{:S(2)}, u32[]{:S(2)}) collective-permute-start(bf16[1,32,4096]{2,1,0:T(8,128)(2,1)S(1)} %bitcast.34), channel_id=1, source_target_pairs={{8,0},{16,8},{24,16},{32,24},{40,32},{48,40},{56,48},{64,56},{72,6... | collective-permute-start | bytes 786440 | tf_op jit(solution)/shard_map/bwd_out/ppermute | solution.py:30
  (16 other events, 204.2 us)

commit v4 on v3

--- a/solution.py
+++ b/solution.py
@@ -281,8 +281,10 @@
     return jnp.where(is_early, early, block)
 
 
-def payload_kernel(slots, x, held, out):
-    out[...] = chosen(slots, 0, x[0], held)
+def first_kernel(slots, x, held, gain, payload_out, normed_out):
+    block = x[0]
+    payload_out[...] = chosen(slots, 0, block, held)
+    normed_out[...] = (unit_rows(block)[0] * gain[...]).astype(BF16)
 
 
 def checkpoint_kernel(slots, received, held, gain, block_out, normed_out):
@@ -304,14 +306,6 @@
     wide = block.astype(F32)
     scale = lax.rsqrt(jnp.mean(wide * wide, axis=-1, keepdims=True) + EPS)
     return wide * scale, scale
-
-
-def norm_kernel(block, gain, out):
-    out[...] = (unit_rows(block[...])[0] * gain[...]).astype(BF16)
-
-
-def normalize(block, gain):
-    return call(norm_kernel, [(block.shape, BF16)], [], [], [block, gain], [], 1)[0]
 
 
 def norm_back_kernel(kept, near, far, block, gain, upstream, out):
@@ -350,10 +344,8 @@
             return core_swap(value)
 
     with jax.named_scope("payload"):
-        payload = with_slots(payload_kernel, [x_fwd.shape[1:]], slot_table, x_fwd, stash)[0]
+        payload, own1 = with_slots(first_kernel, [x_fwd.shape[1:]] * 2, slot_table, x_fwd, stash, norm_gain)
         received = lax.ppermute(payload, "section", [(i, sections - 1 - i) for i in range(sections)])
-    with jax.named_scope("norm_fwd"):
-        own1 = normalize(after(x_fwd[0], payload), norm_gain)
     far1 = send(own1, 2, "g1_far")
     near1 = send(own1, 1, "g1_near")
     last1 = send(far1, 1, "g1_last")

time: 147 us -> 145 us (0.986)
  local copies, waits for them, and re-layouts: 4.83 us -> 8.25 us
  other arithmetic: 6.92 us -> 4.08 us
  waiting for transfers between devices: 72.6 us -> 69.8 us
    ppermute x1, waiting for transfers between devices: 13 us -> 10.9 us  [body(): lax.ppermute(payload, 'section', [(i, sections - 1 - i) for i in range(se...]
    unnamed x31 -> x33, local copies, waits for them, and re-layouts: 4.65 us -> 6.37 us
    concatenate x0 -> x1, local copies, waits for them, and re-layouts: none -> 1.69 us  [body(): mine = jnp.concatenate([own1, far1, near1], axis=0)]
    pallas_call x7 -> x6, Pallas kernels: 18 us -> 17.9 us  [call(): pl.pallas_call(kernel, out_shape=[jax.ShapeDtypeStruct(shape, dtype) for...]
  transfers between devices with their start and end apart: 26 -> 26, of which waited for: 15 -> 15; matrix products, arithmetic and copies ran while one was open for 8% -> 10% of each run, Pallas kernels for 14% -> 14%
where the time goes in v4:
time: 145 us; the launch traced here: 144 us
  waiting for transfers between devices  69.8 us (48%)
  starting transfers between devices  34.6 us (24%)
  Pallas kernels  21.9 us (15%)
  local copies, waits for them, and re-layouts  8.25 us (6%)
  matrix products  4.72 us (3%)
  other arithmetic  4.08 us (3%)
    ppermute x14, waiting for transfers between devices, chip_swap(): lax.ppermute(value, 'tensor', [(i, i ^ 2 * mask) for i in range(size)])  39 us
    ppermute x14, starting transfers between devices, chip_swap(): lax.ppermute(value, 'tensor', [(i, i ^ 2 * mask) for i in range(size)])  22.3 us
    ppermute x1, waiting for transfers between devices, shifted(): lax.ppermute(value, 'section', [(i, i + steps) for i in range(count) if 0...  18.7 us
    pallas_call x6, Pallas kernels, call(): pl.pallas_call(kernel, out_shape=[jax.ShapeDtypeStruct(shape, dtype) for...  17.9 us
    ppermute x1, waiting for transfers between devices, body(): lax.ppermute(payload, 'section', [(i, sections - 1 - i) for i in range(se...  10.9 us
    unnamed x33, local copies, waits for them, and re-layouts  6.37 us
    ppermute x1, starting transfers between devices, body(): lax.ppermute(payload, 'section', [(i, sections - 1 - i) for i in range(se...  4.96 us
    dot_general x6, matrix products, back_project(): return jnp.einsum('tq,dq->td', grads, weight, preferred_element_type=F32)  4.72 us
  transfers between devices with their start and end apart: 26, of which 15 were waited for; matrix products, arithmetic and copies ran while one was open for 10% of the time, Pallas kernels for 14%

profile of v4, /device:TPU:62, one launch (start us, length us, event | category | flops | bytes accessed | tf_op | source)
XLA Modules:
  0.0 144.4 jit_solution(9442855034636785504)
XLA Ops:
  0.6 2.1 %payload.1 = (bf16[32,4096]{1,0:T(8,128)(2,1)}, bf16[32,4096]{1,0:T(8,128)(2,1)}) custom-call(s32[1,2]{1,0:T(1,128)} %slots.3, bf16[1,32,4096]{2,1,0:T(8,128)(2,1)} %x.1, bf16[1,2,32,4096]{3,2,1,0:T(8,128)(2,1)} %held.3, f32[1,4096]{1,0:T(1,128)} %gain.5), custom_call_target="tpu_custom_call" | custom-call | tf_op jit(solution)/shard_map/payload/pallas_call | solution.py:297
  2.7 3.3 %collective-permute-start = (bf16[32,4096]{1,0:T(8,128)(2,1)}, bf16[32,4096]{1,0:T(8,128)(2,1)}, u32[]{:S(2)}, u32[]{:S(2)}) collective-permute-start(bf16[32,4096]{1,0:T(8,128)(2,1)} %get-tuple-element.33), channel_id=1, source_target_pairs={{0,4},{1,5},{2,6},{3,7},{4,0},{5,1},{6,2},{7,3},{8,12},{9,13},{10,... | collective-permute-start | bytes 786440 | tf_op jit(solution)/shard_map/g1_far/ppermute | solution.py:25
  6.1 5.0 %collective-permute-start.2 = (bf16[32,4096]{1,0:T(8,128)(2,1)}, bf16[32,4096]{1,0:T(8,128)(2,1)S(1)}, u32[]{:S(2)}, u32[]{:S(2)}) collective-permute-start(bf16[32,4096]{1,0:T(8,128)(2,1)} %get-tuple-element.34), channel_id=1, source_target_pairs={{0,248},{8,240},{16,232},{24,224},{32,216},{40,208},{48,200},{56,1... | collective-permute-start | bytes 786440 | tf_op jit(solution)/shard_map/payload/ppermute | solution.py:348
  15.1 3.9 %collective-permute-done = bf16[32,4096]{1,0:T(8,128)(2,1)} collective-permute-done((bf16[32,4096]{1,0:T(8,128)(2,1)}, bf16[32,4096]{1,0:T(8,128)(2,1)}, u32[]{:S(2)}, u32[]{:S(2)}) %collective-permute-start) | collective-permute-done | bytes 262176 | tf_op jit(solution)/shard_map/g1_far/ppermute | solution.py:25
  23.7 10.9 %collective-permute-done.2.received = bf16[32,4096]{1,0:T(8,128)(2,1)S(1)} collective-permute-done((bf16[32,4096]{1,0:T(8,128)(2,1)}, bf16[32,4096]{1,0:T(8,128)(2,1)S(1)}, u32[]{:S(2)}, u32[]{:S(2)}) %collective-permute-start.2) | collective-permute-done | bytes 262176 | tf_op jit(solution)/shard_map/payload/ppermute | solution.py:348
  34.6 5.0 %collective-permute-done.3 = bf16[32,4096]{1,0:T(8,128)(2,1)S(1)} collective-permute-done((bf16[32,4096]{1,0:T(8,128)(2,1)}, bf16[32,4096]{1,0:T(8,128)(2,1)S(1)}, u32[]{:S(2)}, u32[]{:S(2)}) %collective-permute-start.3) | collective-permute-done | bytes 262176 | tf_op jit(solution)/shard_map/g2_far/ppermute | solution.py:25
  42.7 2.0 %norm_bwd.1 = (bf16[32,4096]{1,0:T(8,128)(2,1)}, bf16[32,4096]{1,0:T(8,128)(2,1)}) custom-call(s32[1,2]{1,0:T(1,128)} %slots.3, bf16[32,4096]{1,0:T(8,128)(2,1)} %copy-done.9, bf16[1,2,32,4096]{3,2,1,0:T(8,128)(2,1)} %held.3, f32[1,4096]{1,0:T(1,128)} %gain.5), custom_call_target="tpu_custom_call" | custom-call | tf_op jit(solution)/shard_map/norm_bwd/pallas_call | solution.py:297
  45.7 5.2 %collective-permute-start.9 = (bf16[32,4096]{1,0:T(8,128)(2,1)}, bf16[32,4096]{1,0:T(8,128)(2,1)S(1)}, u32[]{:S(2)}, u32[]{:S(2)}) collective-permute-start(bf16[32,4096]{1,0:T(8,128)(2,1)} %get-tuple-element.36), channel_id=1, source_target_pairs={{0,4},{1,5},{2,6},{3,7},{4,0},{5,1},{6,2},{7,3},{8,12},{9,13},{10,... | collective-permute-start | bytes 786440 | tf_op jit(solution)/shard_map/g3_far/ppermute | solution.py:25
  50.9 2.2 %copy-done = bf16[1,4096,512]{2,1,0:T(8,128)(2,1)S(1)} copy-done((bf16[1,4096,512]{2,1,0:T(8,128)(2,1)S(1)}, bf16[1,4096,512]{2,1,0:T(8,128)(2,1)}, u32[]{:S(2)}) %copy-start) | copy-done | bytes 4194328
  53.1 4.7 %qkv_fwd.1 = (bf16[256,512]{1,0:T(8,128)(2,1)S(1)}, bf16[256,128]{1,0:T(8,128)(2,1)S(1)}, bf16[256,128]{1,0:T(8,128)(2,1)S(1)}) custom-call(bf16[96,4096]{1,0:T(8,128)(2,1)} %constant_dynamic-update-slice_fusion.refs_0_, bf16[32,4096]{1,0:T(8,128)(2,1)} %collective-permute-done.4.refs_1_, bf16[96,4096]{1,0:T(8,128)(2,1)} %collective-permute-done.5.refs_2_, ...), custom_call_target="tpu_custom_call" | custom-call | flops 25165824 | bytes 65536 | tf_op jit(solution)/shard_map/qkv_fwd/pallas_call | solution.py:190
  57.9 2.8 %attn_fwd.1 = (f32[128,4096]{1,0:T(8,128)S(1)}, bf16[128,4096]{1,0:T(8,128)(2,1)S(1)}) custom-call(bf16[1,512,4096]{2,1,0:T(8,128)(2,1)S(1)} %copy-done.3, bf16[256,512]{1,0:T(8,128)(2,1)S(1)} %get-tuple-element.38.q, bf16[256,128]{1,0:T(8,128)(2,1)S(1)} %get-tuple-element.39.k, bf16[256,128]{1,0:T(8,128)(2,1)S(1)} %get-tuple-element.40.v, ...), custom_call_target="tpu_custom_call" | custom-call | flops 16777216 | bytes 65536 | tf_op jit(solution)/shard_map/attn_fwd/pallas_call | solution.py:190
  61.5 4.3 %collective-permute-done.10 = bf16[32,4096]{1,0:T(8,128)(2,1)S(1)} collective-permute-done((bf16[32,4096]{1,0:T(8,128)(2,1)}, bf16[32,4096]{1,0:T(8,128)(2,1)S(1)}, u32[]{:S(2)}, u32[]{:S(2)}) %collective-permute-start.10) | collective-permute-done | bytes 262176 | tf_op jit(solution)/shard_map/g3_near/ppermute | solution.py:25
  65.8 4.8 %collective-permute-done.9 = bf16[32,4096]{1,0:T(8,128)(2,1)S(1)} collective-permute-done((bf16[32,4096]{1,0:T(8,128)(2,1)}, bf16[32,4096]{1,0:T(8,128)(2,1)S(1)}, u32[]{:S(2)}, u32[]{:S(2)}) %collective-permute-start.9) | collective-permute-done | bytes 262176 | tf_op jit(solution)/shard_map/g3_far/ppermute | solution.py:25
  71.3 2.1 %collective-permute-start.8 = (bf16[32,4096]{1,0:T(8,128)(2,1)S(1)}, bf16[32,4096]{1,0:T(8,128)(2,1)S(1)}, u32[]{:S(2)}, u32[]{:S(2)}) collective-permute-start(bf16[32,4096]{1,0:T(8,128)(2,1)S(1)} %add_convert_fusion.1), channel_id=1, source_target_pairs={{0,2},{1,3},{2,0},{3,1},{4,6},{5,7},{6,4},{7,5},{8,10},{9,11},{10,... | collective-permute-start | bytes 786440 | tf_op jit(solution)/shard_map/r1_pass/ppermute | solution.py:25
  74.0 3.8 %grad_mixed.1.gm = bf16[256,512]{1,0:T(8,128)(2,1)S(1)} custom-call(bf16[64,4096]{1,0:T(8,128)(2,1)S(1)} %pad_maximum_fusion.refs_0_, bf16[64,4096]{1,0:T(8,128)(2,1)} %collective-permute-done.11.refs_1_, bf16[64,4096]{1,0:T(8,128)(2,1)S(1)} %collective-permute-done.13.refs_2_, bf16[64,4096]{1,0:T(8,128)(2,1)S(1)} %collective-permute-done.14.refs_3_, ...), custom_call_target="tpu_custom_call" | custom-call | flops 16777216 | bytes 65536 | tf_op jit(solution)/shard_map/grad_mixed/pallas_call | solution.py:190
  79.8 4.6 %collective-permute-done.8 = bf16[32,4096]{1,0:T(8,128)(2,1)S(1)} collective-permute-done((bf16[32,4096]{1,0:T(8,128)(2,1)S(1)}, bf16[32,4096]{1,0:T(8,128)(2,1)S(1)}, u32[]{:S(2)}, u32[]{:S(2)}) %collective-permute-start.8) | collective-permute-done | bytes 262176 | tf_op jit(solution)/shard_map/r1_pass/ppermute | solution.py:25
  86.4 3.8 %qkv_bwd.1 = (bf16[256,512]{1,0:T(8,128)(2,1)S(1)}, bf16[256,128]{1,0:T(8,128)(2,1)S(1)}, bf16[256,128]{1,0:T(8,128)(2,1)S(1)}) custom-call(bf16[96,4096]{1,0:T(8,128)(2,1)S(1)} %constant_dynamic-update-slice_fusion.3.refs_0_, bf16[32,4096]{1,0:T(8,128)(2,1)S(1)} %collective-permute-done.12.refs_1_, bf16[96,4096]{1,0:T(8,128)(2,1)S(1)} %collective-permute-done.16.refs_2_, ...), custom_call_target="tpu_custom_call" | custom-call | flops 25165824 | bytes 65536 | tf_op jit(solution)/shard_map/qkv_bwd/pallas_call | solution.py:190
  90.3 2.3 %attn_bwd.1 = (bf16[256,512]{1,0:T(8,128)(2,1)S(1)}, bf16[256,128]{1,0:T(8,128)(2,1)S(1)}, bf16[256,128]{1,0:T(8,128)(2,1)S(1)}) custom-call(bf16[256,512]{1,0:T(8,128)(2,1)S(1)} %get-tuple-element.52.q, bf16[256,128]{1,0:T(8,128)(2,1)S(1)} %get-tuple-element.53.k, bf16[256,128]{1,0:T(8,128)(2,1)S(1)} %get-tuple-element.54.v, ...), custom_call_target="tpu_custom_call" | custom-call | flops 8388608 | bytes 65536 | tf_op jit(solution)/shard_map/attn_bwd/pallas_call | solution.py:190
  100.0 2.1 %collective-permute-start.20 = (bf16[1,32,4096]{2,1,0:T(8,128)(2,1)S(1)}, bf16[1,32,4096]{2,1,0:T(8,128)(2,1)S(1)}, u32[]{:S(2)}, u32[]{:S(2)}) collective-permute-start(bf16[1,32,4096]{2,1,0:T(8,128)(2,1)S(1)} %fusion.17), channel_id=1, source_target_pairs={{0,8},{8,16},{16,24},{24,32},{32,40},{40,48},{48,56},{56,64},{64,7... | collective-permute-start | bytes 786440 | tf_op jit(solution)/shard_map/fwd_out/ppermute | solution.py:422
  102.2 4.3 %collective-permute-done.22 = bf16[32,4096]{1,0:T(8,128)(2,1)S(1)} collective-permute-done((bf16[32,4096]{1,0:T(8,128)(2,1)S(1)}, bf16[32,4096]{1,0:T(8,128)(2,1)S(1)}, u32[]{:S(2)}, u32[]{:S(2)}) %collective-permute-start.22) | collective-permute-done | bytes 262176 | tf_op jit(solution)/shard_map/r2_pass/ppermute | solution.py:25
  111.8 7.0 %collective-permute-done.23.near = bf16[32,4096]{1,0:T(8,128)(2,1)S(1)} collective-permute-done((bf16[32,4096]{1,0:T(8,128)(2,1)S(1)}, bf16[32,4096]{1,0:T(8,128)(2,1)S(1)}, u32[]{:S(2)}, u32[]{:S(2)}) %collective-permute-start.23) | collective-permute-done | bytes 262176 | tf_op jit(solution)/shard_map/r2_near/ppermute | solution.py:25
  118.8 2.2 %collective-permute-done.24.far = bf16[32,4096]{1,0:T(8,128)(2,1)S(1)} collective-permute-done((bf16[32,4096]{1,0:T(8,128)(2,1)S(1)}, bf16[32,4096]{1,0:T(8,128)(2,1)S(1)}, u32[]{:S(2)}, u32[]{:S(2)}) %collective-permute-start.24) | collective-permute-done | bytes 262176 | tf_op jit(solution)/shard_map/r2_far/ppermute | solution.py:25
  121.4 2.7 %collective-permute-start.25 = (bf16[1,32,4096]{2,1,0:T(8,128)(2,1)S(1)}, bf16[1,32,4096]{2,1,0:T(8,128)(2,1)S(1)}, u32[]{:S(2)}, u32[]{:S(2)}) collective-permute-start(bf16[1,32,4096]{2,1,0:T(8,128)(2,1)S(1)} %bitcast.34), channel_id=1, source_target_pairs={{8,0},{16,8},{24,16},{32,24},{40,32},{48,40},{56,48},{64,56},{72,6... | collective-permute-start | bytes 786440 | tf_op jit(solution)/shard_map/bwd_out/ppermute | solution.py:30
  124.9 18.7 %collective-permute-done.25 = bf16[1,32,4096]{2,1,0:T(8,128)(2,1)S(1)} collective-permute-done((bf16[1,32,4096]{2,1,0:T(8,128)(2,1)S(1)}, bf16[1,32,4096]{2,1,0:T(8,128)(2,1)S(1)}, u32[]{:S(2)}, u32[]{:S(2)}) %collective-permute-start.25) | collective-permute-done | bytes 262176 | tf_op jit(solution)/shard_map/bwd_out/ppermute | solution.py:30
  (97 shorter events, 33.6 us)
Async XLA Ops:
  2.7 16.3 %collective-permute-start = (bf16[32,4096]{1,0:T(8,128)(2,1)}, bf16[32,4096]{1,0:T(8,128)(2,1)}, u32[]{:S(2)}, u32[]{:S(2)}) collective-permute-start(bf16[32,4096]{1,0:T(8,128)(2,1)} %get-tuple-element.33), channel_id=1, source_target_pairs={{0,4},{1,5},{2,6},{3,7},{4,0},{5,1},{6,2},{7,3},{8,12},{9,13},{10,... | collective-permute-start | bytes 786440 | tf_op jit(solution)/shard_map/g1_far/ppermute | solution.py:25
  6.0 15.9 %collective-permute-start.1 = (bf16[32,4096]{1,0:T(8,128)(2,1)}, bf16[32,4096]{1,0:T(8,128)(2,1)}, u32[]{:S(2)}, u32[]{:S(2)}) collective-permute-start(bf16[32,4096]{1,0:T(8,128)(2,1)} %get-tuple-element.33), channel_id=1, source_target_pairs={{0,2},{1,3},{2,0},{3,1},{4,6},{5,7},{6,4},{7,5},{8,10},{9,11},{10,... | collective-permute-start | bytes 786440 | tf_op jit(solution)/shard_map/g1_near/ppermute | solution.py:25
  6.1 28.5 %collective-permute-start.2 = (bf16[32,4096]{1,0:T(8,128)(2,1)}, bf16[32,4096]{1,0:T(8,128)(2,1)S(1)}, u32[]{:S(2)}, u32[]{:S(2)}) collective-permute-start(bf16[32,4096]{1,0:T(8,128)(2,1)} %get-tuple-element.34), channel_id=1, source_target_pairs={{0,248},{8,240},{16,232},{24,224},{32,216},{40,208},{48,200},{56,1... | collective-permute-start | bytes 786440 | tf_op jit(solution)/shard_map/payload/ppermute | solution.py:348
  11.0 28.5 %collective-permute-start.3 = (bf16[32,4096]{1,0:T(8,128)(2,1)}, bf16[32,4096]{1,0:T(8,128)(2,1)S(1)}, u32[]{:S(2)}, u32[]{:S(2)}) collective-permute-start(bf16[32,4096]{1,0:T(8,128)(2,1)} %bitcast.32), channel_id=1, source_target_pairs={{0,4},{1,5},{2,6},{3,7},{4,0},{5,1},{6,2},{7,3},{8,12},{9,13},{10,... | collective-permute-start | bytes 786440 | tf_op jit(solution)/shard_map/g2_far/ppermute | solution.py:25
  19.0 21.5 %collective-permute-start.4 = (bf16[32,4096]{1,0:T(8,128)(2,1)}, bf16[32,4096]{1,0:T(8,128)(2,1)}, u32[]{:S(2)}, u32[]{:S(2)}) collective-permute-start(bf16[32,4096]{1,0:T(8,128)(2,1)} %collective-permute-done), channel_id=1, source_target_pairs={{0,2},{1,3},{2,0},{3,1},{4,6},{5,7},{6,4},{7,5},{8,10},{9,11},{10,... | collective-permute-start | bytes 786440 | tf_op jit(solution)/shard_map/g1_last/ppermute | solution.py:25
  23.6 27.3 %collective-permute-start.5 = (bf16[96,4096]{1,0:T(8,128)(2,1)}, bf16[96,4096]{1,0:T(8,128)(2,1)}, u32[]{:S(2)}, u32[]{:S(2)}) collective-permute-start(bf16[96,4096]{1,0:T(8,128)(2,1)} %constant_dynamic-update-slice_fusion.refs_0_), channel_id=1, source_target_pairs={{0,1},{1,0},{2,3},{3,2},{4,5},{5,4},{6,7},{7,6},{8,9},{9,8},{10,11... | collective-permute-start | bytes 2359304 | tf_op jit(solution)/shard_map/qkv_fwd/g1_swap/ppermute | solution.py:20
  40.6 10.4 %collective-permute-start.6 = (bf16[32,4096]{1,0:T(8,128)(2,1)}, bf16[32,4096]{1,0:T(8,128)(2,1)}, u32[]{:S(2)}, u32[]{:S(2)}) collective-permute-start(bf16[32,4096]{1,0:T(8,128)(2,1)} %collective-permute-done.4.refs_1_), channel_id=1, source_target_pairs={{0,1},{1,0},{2,3},{3,2},{4,5},{5,4},{6,7},{7,6},{8,9},{9,8},{10,11... | collective-permute-start | bytes 786440 | tf_op jit(solution)/shard_map/qkv_fwd/g1_swaplast/ppermute | solution.py:20
  41.6 29.1 %collective-permute-start.11 = (bf16[64,4096]{1,0:T(8,128)(2,1)S(1)}, bf16[64,4096]{1,0:T(8,128)(2,1)}, u32[]{:S(2)}, u32[]{:S(2)}) collective-permute-start(bf16[64,4096]{1,0:T(8,128)(2,1)S(1)} %pad_maximum_fusion.refs_0_), channel_id=1, source_target_pairs={{0,2},{1,3},{2,0},{3,1},{4,6},{5,7},{6,4},{7,5},{8,10},{9,11},{10,... | collective-permute-start | bytes 1572872 | tf_op jit(solution)/shard_map/g2_near/ppermute | solution.py:25
  44.7 21.1 %collective-permute-start.10 = (bf16[32,4096]{1,0:T(8,128)(2,1)}, bf16[32,4096]{1,0:T(8,128)(2,1)S(1)}, u32[]{:S(2)}, u32[]{:S(2)}) collective-permute-start(bf16[32,4096]{1,0:T(8,128)(2,1)} %get-tuple-element.36), channel_id=1, source_target_pairs={{0,2},{1,3},{2,0},{3,1},{4,6},{5,7},{6,4},{7,5},{8,10},{9,11},{10,... | collective-permute-start | bytes 786440 | tf_op jit(solution)/shard_map/g3_near/ppermute | solution.py:25
  45.7 24.9 %collective-permute-start.9 = (bf16[32,4096]{1,0:T(8,128)(2,1)}, bf16[32,4096]{1,0:T(8,128)(2,1)S(1)}, u32[]{:S(2)}, u32[]{:S(2)}) collective-permute-start(bf16[32,4096]{1,0:T(8,128)(2,1)} %get-tuple-element.36), channel_id=1, source_target_pairs={{0,4},{1,5},{2,6},{3,7},{4,0},{5,1},{6,2},{7,3},{8,12},{9,13},{10,... | collective-permute-start | bytes 786440 | tf_op jit(solution)/shard_map/g3_far/ppermute | solution.py:25
  60.6 10.7 %collective-permute-start.7 = (bf16[128,4096]{1,0:T(8,128)(2,1)S(1)}, bf16[128,4096]{1,0:T(8,128)(2,1)S(1)}, u32[]{:S(2)}, u32[]{:S(2)}) collective-permute-start(bf16[128,4096]{1,0:T(8,128)(2,1)S(1)} %get-tuple-element.42), channel_id=1, source_target_pairs={{0,1},{1,0},{2,3},{3,2},{4,5},{5,4},{6,7},{7,6},{8,9},{9,8},{10,11... | collective-permute-start | bytes 3145736 | tf_op jit(solution)/shard_map/r1_swap/ppermute | solution.py:20
  60.8 12.8 %collective-permute-start.13 = (bf16[64,4096]{1,0:T(8,128)(2,1)S(1)}, bf16[64,4096]{1,0:T(8,128)(2,1)S(1)}, u32[]{:S(2)}, u32[]{:S(2)}) collective-permute-start(bf16[64,4096]{1,0:T(8,128)(2,1)S(1)} %pad_maximum_fusion.refs_0_), channel_id=1, source_target_pairs={{0,1},{1,0},{2,3},{3,2},{4,5},{5,4},{6,7},{7,6},{8,9},{9,8},{10,11... | collective-permute-start | bytes 1572872 | tf_op jit(solution)/shard_map/grad_mixed/g2_swap/ppermute | solution.py:20
  70.6 9.2 %collective-permute-start.12 = (bf16[32,4096]{1,0:T(8,128)(2,1)S(1)}, bf16[32,4096]{1,0:T(8,128)(2,1)S(1)}, u32[]{:S(2)}, u32[]{:S(2)}) collective-permute-start(bf16[32,4096]{1,0:T(8,128)(2,1)S(1)} %collective-permute-done.9), channel_id=1, source_target_pairs={{0,2},{1,3},{2,0},{3,1},{4,6},{5,7},{6,4},{7,5},{8,10},{9,11},{10,... | collective-permute-start | bytes 786440 | tf_op jit(solution)/shard_map/g3_last/ppermute | solution.py:25
  70.7 15.7 %collective-permute-start.16 = (bf16[96,4096]{1,0:T(8,128)(2,1)S(1)}, bf16[96,4096]{1,0:T(8,128)(2,1)S(1)}, u32[]{:S(2)}, u32[]{:S(2)}) collective-permute-start(bf16[96,4096]{1,0:T(8,128)(2,1)S(1)} %constant_dynamic-update-slice_fusion.3.refs_0_), channel_id=1, source_target_pairs={{0,1},{1,0},{2,3},{3,2},{4,5},{5,4},{6,7},{7,6},{8,9},{9,8},{10,11... | collective-permute-start | bytes 2359304 | tf_op jit(solution)/shard_map/qkv_bwd/g3_swap/ppermute | solution.py:20
  70.8 3.2 %collective-permute-start.14 = (bf16[64,4096]{1,0:T(8,128)(2,1)}, bf16[64,4096]{1,0:T(8,128)(2,1)S(1)}, u32[]{:S(2)}, u32[]{:S(2)}) collective-permute-start(bf16[64,4096]{1,0:T(8,128)(2,1)} %collective-permute-done.11.refs_1_), channel_id=1, source_target_pairs={{0,1},{1,0},{2,3},{3,2},{4,5},{5,4},{6,7},{7,6},{8,9},{9,8},{10,11... | collective-permute-start | bytes 1572872 | tf_op jit(solution)/shard_map/grad_mixed/g2_swapnear/ppermute | solution.py:20
  71.3 13.0 %collective-permute-start.8 = (bf16[32,4096]{1,0:T(8,128)(2,1)S(1)}, bf16[32,4096]{1,0:T(8,128)(2,1)S(1)}, u32[]{:S(2)}, u32[]{:S(2)}) collective-permute-start(bf16[32,4096]{1,0:T(8,128)(2,1)S(1)} %add_convert_fusion.1), channel_id=1, source_target_pairs={{0,2},{1,3},{2,0},{3,1},{4,6},{5,7},{6,4},{7,5},{8,10},{9,11},{10,... | collective-permute-start | bytes 786440 | tf_op jit(solution)/shard_map/r1_pass/ppermute | solution.py:25
  84.4 15.4 %collective-permute-start.15 = (bf16[32,4096]{1,0:T(8,128)(2,1)S(1)}, bf16[32,4096]{1,0:T(8,128)(2,1)S(1)}, u32[]{:S(2)}, u32[]{:S(2)}) collective-permute-start(bf16[32,4096]{1,0:T(8,128)(2,1)S(1)} %convert_add_fusion.1), channel_id=1, source_target_pairs={{0,2},{1,3},{2,0},{3,1},{4,6},{5,7},{6,4},{7,5},{8,10},{9,11},{10,... | collective-permute-start | bytes 786440 | tf_op jit(solution)/shard_map/r1_near/ppermute | solution.py:25
  84.8 15.0 %collective-permute-start.19 = (bf16[32,4096]{1,0:T(8,128)(2,1)S(1)}, bf16[32,4096]{1,0:T(8,128)(2,1)S(1)}, u32[]{:S(2)}, u32[]{:S(2)}) collective-permute-start(bf16[32,4096]{1,0:T(8,128)(2,1)S(1)} %add_convert_fusion), channel_id=1, source_target_pairs={{0,4},{1,5},{2,6},{3,7},{4,0},{5,1},{6,2},{7,3},{8,12},{9,13},{10,... | collective-permute-start | bytes 786440 | tf_op jit(solution)/shard_map/r1_far/ppermute | solution.py:25
  98.0 8.6 %collective-permute-start.22 = (bf16[32,4096]{1,0:T(8,128)(2,1)S(1)}, bf16[32,4096]{1,0:T(8,128)(2,1)S(1)}, u32[]{:S(2)}, u32[]{:S(2)}) collective-permute-start(bf16[32,4096]{1,0:T(8,128)(2,1)S(1)} %fusion.15), channel_id=1, source_target_pairs={{0,2},{1,3},{2,0},{3,1},{4,6},{5,7},{6,4},{7,5},{8,10},{9,11},{10,... | collective-permute-start | bytes 786440 | tf_op jit(solution)/shard_map/r2_pass/ppermute | solution.py:25
  100.0 10.2 %collective-permute-start.20 = (bf16[1,32,4096]{2,1,0:T(8,128)(2,1)S(1)}, bf16[1,32,4096]{2,1,0:T(8,128)(2,1)S(1)}, u32[]{:S(2)}, u32[]{:S(2)}) collective-permute-start(bf16[1,32,4096]{2,1,0:T(8,128)(2,1)S(1)} %fusion.17), channel_id=1, source_target_pairs={{0,8},{8,16},{16,24},{24,32},{32,40},{40,48},{48,56},{56,64},{64,7... | collective-permute-start | bytes 786440 | tf_op jit(solution)/shard_map/fwd_out/ppermute | solution.py:422
  106.5 12.3 %collective-permute-start.23 = (bf16[32,4096]{1,0:T(8,128)(2,1)S(1)}, bf16[32,4096]{1,0:T(8,128)(2,1)S(1)}, u32[]{:S(2)}, u32[]{:S(2)}) collective-permute-start(bf16[32,4096]{1,0:T(8,128)(2,1)S(1)} %slice_add_fusion.1), channel_id=1, source_target_pairs={{0,2},{1,3},{2,0},{3,1},{4,6},{5,7},{6,4},{7,5},{8,10},{9,11},{10,... | collective-permute-start | bytes 786440 | tf_op jit(solution)/shard_map/r2_near/ppermute | solution.py:25
  108.4 12.6 %collective-permute-start.24 = (bf16[32,4096]{1,0:T(8,128)(2,1)S(1)}, bf16[32,4096]{1,0:T(8,128)(2,1)S(1)}, u32[]{:S(2)}, u32[]{:S(2)}) collective-permute-start(bf16[32,4096]{1,0:T(8,128)(2,1)S(1)} %get-tuple-element.63), channel_id=1, source_target_pairs={{0,4},{1,5},{2,6},{3,7},{4,0},{5,1},{6,2},{7,3},{8,12},{9,13},{10,... | collective-permute-start | bytes 786440 | tf_op jit(solution)/shard_map/r2_far/ppermute | solution.py:25
  110.2 14.0 %collective-permute-start.21 = (bf16[1,32,4096]{2,1,0:T(8,128)(2,1)S(1)}, bf16[1,32,4096]{2,1,0:T(8,128)(2,1)S(1)}, u32[]{:S(2)}, u32[]{:S(2)}) collective-permute-start(bf16[1,32,4096]{2,1,0:T(8,128)(2,1)S(1)} %collective-permute-done.20), channel_id=1, source_target_pairs={{0,128},{1,129},{2,130},{3,131},{4,132},{5,133},{6,134},{7,135}} | collective-permute-start | bytes 786440 | tf_op jit(solution)/shard_map/fwd_out/ppermute | solution.py:423
  121.4 22.2 %collective-permute-start.25 = (bf16[1,32,4096]{2,1,0:T(8,128)(2,1)S(1)}, bf16[1,32,4096]{2,1,0:T(8,128)(2,1)S(1)}, u32[]{:S(2)}, u32[]{:S(2)}) collective-permute-start(bf16[1,32,4096]{2,1,0:T(8,128)(2,1)S(1)} %bitcast.34), channel_id=1, source_target_pairs={{8,0},{16,8},{24,16},{32,24},{40,32},{48,40},{56,48},{64,56},{72,6... | collective-permute-start | bytes 786440 | tf_op jit(solution)/shard_map/bwd_out/ppermute | solution.py:30
  (16 other events, 212.5 us)
